TPU v7x, 32 devices: a whole 2x2x4 slice. The times are simulated.
32 devices in a mesh: gx: 16 (over z, y, x), gy: 2 (over core).
Axes of the slice: x: 2, y: 2, z: 4, core: 2. Of those that a mesh axis runs over, the one named last changes fastest.
Arguments:
- velocity: float32 [512, 64, 128], P('gx', 'gy'), may hold values from -6 to 6
Outputs:
- coefficients: float32 [512, 64, 128], P('gx', 'gy')
All inputs are finite; a program needn't handle non-finite values.
Results may differ from a plain program's by a relative error of at most 0.00002.
Values sent between devices are 32-bit elements; how exact they have to be, the bound alone decides.
No kernel may reach another device: no remote copies, remote signals or barrier semaphores. Data moves between devices by JAX's collectives and lax.ppermute only.
A program may use at most 128 MiB of HBM per device.

v0:
```python
import functools

import jax
import jax.numpy as jnp
import numpy as np
from jax import lax
from jax.experimental import pallas as pl
from jax.experimental.pallas import tpu as pltpu
from jax.sharding import PartitionSpec as P

LEVELS = 4
STEPS = (-1.586134342, -0.05298011854, 0.8829110762, 0.4435068522)
SCALE = 1.149604398
VMEM_BYTES = 24 * 2**20
FIRST_FLOPS = 10**10
SHARED = True


def windows(block):
    found = []
    first, last = 0, block - 1
    for _ in range(LEVELS):
        low = first - 4 + (first % 2)
        high = last + 4 - (last % 2)
        found.append((low, high))
        first, last = low // 2, high // 2
    return found


def message(block, rows, to):
    sent, derived = {}, {}
    spans = windows(block)
    base = ends = 0
    for level, (low, high) in enumerate(spans):
        size, height = block >> level, rows >> level
        first, last = (0, block - 1) if level == 0 else (v // 2 for v in spans[level - 1])
        planes = [p for p in range(low, high + 1) if p // size == to]
        if abs(to) == 1:
            sign = to
            edge = last + 2 - last % 2 if to > 0 else first - 2 + first % 2
            far, near = edge + sign, edge - sign
            if far in planes and edge + 2 * sign in planes:
                derived[level, edge + 2 * sign] = (far, None)
            if far in planes and near in planes:
                derived[level, edge] = (far, near)
        planes = [plane for plane in planes if (level, plane) not in derived]
        at = base
        if level == 1:
            extra = planes[-1] if len(planes) > 3 else None
        elif level > 1 and extra is not None:
            at = base + (rows >> 1)
        for plane in planes:
            if level == 1 and plane == extra:
                sent[level, plane] = base, shift_of(2)
                continue
            sent[level, plane] = at, shift_of(level)
            at += height
        ends = max(ends, at)
        if level == 0:
            base = at
    return sent, derived, -(-ends // 8) * 8


def shift_of(level):
    return (0, 0, 1, 3)[level]


def places_of(block):
    found = set()
    for level, (low, high) in enumerate(windows(block)):
        size = block >> level
        found |= set(range(low // size, high // size + 1))
    return sorted(found - {0})


def z_product(value, weights):
    width = value.shape[-1]
    high = value.astype(jnp.bfloat16)
    rest = (value - high.astype(jnp.float32)).astype(jnp.bfloat16)
    both = jnp.concatenate([high, rest], axis=1)
    product = jnp.dot(both, weights, preferred_element_type=jnp.float32)
    return product[:, :width] + product[:, width:]


def lanes_of(width, spacing, parity):
    lane = lax.broadcasted_iota(jnp.int32, (1, width), 1)
    return lax.rem(lane, 2 * spacing) == (spacing if parity else 0)


def own_lanes(width, level, high_only):
    spacing, shift = 1 << level, shift_of(level)
    lane = lax.broadcasted_iota(jnp.int32, (1, width), 1)
    if high_only:
        return lax.rem(lane, 2 * spacing) == spacing + shift
    return lax.rem(lane, spacing) == shift


def z_lift(value, spacing):
    width = value.shape[-1]
    axis = value.ndim - 1
    for step, weight in enumerate(STEPS):
        factor = jnp.where(lanes_of(width, spacing, step % 2 == 0), weight, 0.0)
        around = pltpu.roll(value, spacing, axis) + pltpu.roll(value, width - spacing, axis)
        value = value + factor * around
    return value


def x_lift(planes):
    def plus(one, other):
        return other if one is None else one if other is None else one + other

    planes = dict(planes)
    for step, weight in enumerate(STEPS):
        parity = 1 if step % 2 == 0 else 0
        for index in range(min(planes) - 1, max(planes) + 2):
            if index % 2 == parity:
                around = plus(planes.get(index - 1), planes.get(index + 1))
                if around is not None:
                    planes[index] = plus(planes.get(index), weight * around)
    return planes


def y_lift_split(even, odd):
    count = even.shape[0]
    a, b, c, d = STEPS
    odd = odd + a * (even + pltpu.roll(even, count - 1, 0))
    even = even + b * (pltpu.roll(odd, 1, 0) + odd)
    odd = odd + c * (even + pltpu.roll(even, count - 1, 0))
    even = even + d * (pltpu.roll(odd, 1, 0) + odd)
    return even, odd


def y_lift_whole(value):
    count = value.shape[0]
    row = lax.broadcasted_iota(jnp.int32, (count, 1), 0)
    for step, weight in enumerate(STEPS):
        factor = jnp.where(lax.rem(row, 2) == (1 if step % 2 == 0 else 0), weight, 0.0)
        value = value + factor * (pltpu.roll(value, 1, 0) + pltpu.roll(value, count - 1, 0))
    return value


def scaled_z(value, spacing):
    width = value.shape[-1]
    odd, even = lanes_of(width, spacing, True), lanes_of(width, spacing, False)
    return value * jnp.where(odd, SCALE, jnp.where(even, 1 / SCALE, 0.0))


def scaled(value, x_odd, y_odd):
    at = (SCALE if x_odd else 1 / SCALE) * (SCALE if y_odd else 1 / SCALE)
    return value if x_odd != y_odd else value * at


def spread_z(source, weights, spread, rows, start, size):
    width = source.shape[-1]
    value = source[start : start + size].reshape(size * rows, width)
    spread[start * rows : (start + size) * rows, :] = z_product(value, weights[...])


def spread_x(block, rows, spread, into, low, base):
    for at in range(0, rows, 8):
        planes = {x: spread[x * rows + at : x * rows + at + 8, :] for x in range(block)}
        for x, value in x_lift(planes).items():
            into[x - low, base + at : base + at + 8, :] = value


def matrix_kernel(*weights):
    width = weights[0].shape[0] // 2
    row = lax.broadcasted_iota(jnp.int32, (width, width), 0)
    lane = lax.broadcasted_iota(jnp.int32, (width, width), 1)
    value = jnp.where(row == lane, 1.0, 0.0)
    full = [scaled_z(z_lift(value, 1), 1), jnp.zeros((width, width), jnp.float32)]
    for level in range(1, LEVELS):
        spacing = 1 << level
        value = scaled_z(z_lift(value, spacing), spacing)
        full[1] += pltpu.roll(value, shift_of(level), 1) if shift_of(level) else value
        value = jnp.where(lanes_of(width, spacing, False), value, 0.0)
    for weight, matrix in zip(weights, full):
        high = matrix.astype(jnp.bfloat16)
        rest = (matrix - high.astype(jnp.float32)).astype(jnp.bfloat16)
        weight[:width, :width] = high
        weight[:width, width:] = rest
        weight[width:, :width] = high
        weight[width:, width:] = jnp.zeros_like(rest)


def own_kernel(block, rows, velocity, weights, into, spread):
    step = max(1, min(block, 512 // rows))
    for x in range(0, block, step):
        spread_z(velocity, weights, spread, rows, x, step)
    spread_x(block, rows, spread, into, windows(block)[0][0], 0)


def right_source(step, place, last):
    return place == last if step == 1 else (place == 0) | (place == last - 1)


def right_target(step, place):
    return (place == 0) & (step == 1)


def sends_right(step):
    core = lax.axis_index("gy") == 1
    return core == right_source(step, lax.axis_index("gx"), lax.axis_size("gx") - 1)


def takes_right(step):
    core = lax.axis_index("gy") == 1
    return core == right_target(step, lax.axis_index("gx"))


def shared_pairs(step, around):
    pairs = []
    for place in range(around):
        to, back = (place + step) % around, (place - step) % around
        source = int(right_source(step, place, around - 1))
        pairs.append((2 * place + source, 2 * to + int(right_target(step, to))))
        pairs.append((2 * place + 1 - source, 2 * back + 1 - int(right_target(step, back))))
    return pairs


def message_kernel(block, rows, width, count, places, *refs):
    refs = list(refs)

    def take(number):
        taken = refs[:number]
        del refs[:number]
        return taken

    shared = count == 2 and SHARED
    halves = 2 if shared else 1
    (_,) = take(1)
    others = take(count - 1)
    weights = take(2)
    lifted = take(LEVELS)
    passed = take(2 if shared else len(places))
    (spread,) = take(1)
    coarse = take(LEVELS - 1)
    both = take(2) if shared else []
    messages = dict(zip(places, passed))
    spans = windows(block)
    total = count * rows
    tables = {to: message(block, rows, to) for to in places}
    lengths = {to: message(block, rows, to)[2] for to in places}
    if shared:
        for step, buffer in enumerate(both, 1):
            size = buffer.shape[0] // 4
            for side, to in enumerate((step, -step)):
                lengths[to] = size
                messages[to] = buffer.at[pl.ds(2 * side * size, 2 * size)]
    written = {to: set() for to in places}

    def post(to, at, number, value):
        here = range(at, at + 2 * number, 2)
        if written[to].isdisjoint(here):
            messages[to][pl.ds(at, number, 2), :] = value
        else:
            messages[to][pl.ds(at, number, 2), :] += value
        written[to].update(here)

    def put(level, plane, half, even, odd):
        number = (rows >> level) // 2
        low = level < LEVELS - 1 and plane % 2 == 0
        if level > 0 or low:
            even = jnp.where(own_lanes(width, level, low), even, 0.0)
        if level > 0:
            odd = jnp.where(own_lanes(width, level, False), odd, 0.0)
        to = plane // (block >> level)
        at, shift = tables[to][0][level, plane]
        at += half * lengths[to]
        if shift != shift_of(level):
            even, odd = (pltpu.roll(value, shift - shift_of(level), 1) for value in (even, odd))
        post(to, at, number, even)
        post(to, at + 1, number, odd)

    for level in range(LEVELS):
        low, high = spans[level]
        height = total >> level
        half, mine = height // 2, (rows >> level) // 2
        into = lifted[level]

        if level == 0:
            for part, source in enumerate(others):
                step = min(block, max(1, 512 // rows))
                for x in range(0, block, step):
                    spread_z(source, weights[0], spread, rows, x, step)
                spread_x(block, rows, spread, into, low, (part + 1) * rows)
        else:
            start, stop = spans[level - 1][0] // 2, spans[level - 1][1] // 2 + 1
            source = coarse[level - 1]
            if level == 1:
                size = (stop - start) * height
                for at in range(0, size, 512):
                    end = min(size, at + 512)
                    source[at:end, :] = z_product(source[at:end, :], weights[level][...])
            for at in range(0, height, 8):
                planes = {}
                for x in range(start, stop):
                    row = (x - start) * height + at
                    planes[x] = source[row : row + 8, :]
                for x, value in x_lift(planes).items():
                    into[x - low, at : at + 8, :] = value

        for plane in range(low, high + 1):
            odd_plane = plane % 2 == 1
            to = plane // (block >> level)
            goes_on = level < LEVELS - 1 and not odd_plane
            sends = to != 0 and (level, plane) in tables[to][0]
            if not goes_on and not sends:
                continue
            at = plane - low
            split = half % 8 == 0
            if split:
                even, odd = y_lift_split(
                    into[at, pl.ds(0, half, 2), :], into[at, pl.ds(1, half, 2), :]
                )
                even = scaled(even, odd_plane, False)
            else:
                into[at] = y_lift_whole(into[at])
                even = scaled(into[at, pl.ds(0, half, 2), :], odd_plane, False)
            if goes_on:
                row = ((plane - low) // 2) * half
                coarse[level][row : row + half, :] = even
            if not sends:
                continue
            for part in range(halves):
                if split:
                    here_even = even[part * mine : (part + 1) * mine]
                    here_odd = odd[part * mine : (part + 1) * mine]
                else:
                    here_even = into[at, pl.ds(2 * part * mine, mine, 2), :]
                    here_even = scaled(here_even, odd_plane, False)
                    here_odd = into[at, pl.ds(2 * part * mine + 1, mine, 2), :]
                put(level, plane, part, here_even, scaled(here_odd, odd_plane, True))

    for to in places:
        for row in range(halves * lengths[to]):
            if row not in written[to]:
                messages[to][row : row + 1, :] = jnp.zeros((1, width), jnp.float32)
    if shared:
        core = lax.axis_index("gy")
        for step, (target, buffer) in enumerate(zip(passed, both), 1):
            size = lengths[step]
            side = jnp.where(sends_right(step), 0, 2 * size)
            for half in range(2):
                here = side + (core if half == 0 else 1 - core) * size
                target[half * size : (half + 1) * size, :] = buffer[pl.ds(pl.multiple_of(here, 8), size), :]


def rest_kernel(block, rows, width, *refs):
    lifted, out, spare = refs[:LEVELS], refs[LEVELS], refs[LEVELS + 1]
    for level, (low, _) in enumerate(windows(block)):
        into, spacing, shift = lifted[level], 1 << level, shift_of(level)
        half, mine = into.shape[1] // 2, (rows >> level) // 2
        for plane in range(block >> level):
            odd_plane = plane % 2 == 1
            at = plane - low
            if half % 8 == 0:
                even, odd = y_lift_split(
                    into[at, pl.ds(0, half, 2), :], into[at, pl.ds(1, half, 2), :]
                )
                even, odd = even[:mine], odd[:mine]
            else:
                spare[plane] = y_lift_whole(into[at])
                even, odd = spare[plane, pl.ds(0, mine, 2), :], spare[plane, pl.ds(1, mine, 2), :]
            even, odd = scaled(even, odd_plane, False), scaled(odd, odd_plane, True)
            further = level < LEVELS - 1 and not odd_plane
            if level > 0 or further:
                even = jnp.where(own_lanes(width, level, further), even, 0.0)
            x = plane * spacing
            if level == 0:
                out[x, pl.ds(0, mine, 2), :] = even
                out[x, pl.ds(1, mine, 2), :] = odd
                continue
            odd = jnp.where(own_lanes(width, level, False), odd, 0.0)
            if shift:
                even, odd = (pltpu.roll(value, width - shift, 1) for value in (even, odd))
            out[x, pl.ds(0, mine, 2 * spacing), :] += even
            out[x, pl.ds(spacing, mine, 2 * spacing), :] += odd


def add_message(block, rows, to, arrived, base, out, clean):
    sent, derived, _ = message(block, rows, to)
    a, b, c, d = STEPS
    width = out.shape[-1]
    lane = lax.broadcasted_iota(jnp.int32, (1, width), 1)
    for level in sorted({level for level, _ in sent}):
        spacing, height = 1 << level, rows >> level
        shape = (height, width)
        held = {}
        for shift in sorted({shift for (found, _), (_, shift) in sent.items() if found == level}):
            here = {
                plane: at for (found, plane), (at, by) in sent.items() if (found, by) == (level, shift)
            }
            start, stop = min(here.values()), -(-(max(here.values()) + height) // 8) * 8
            source, offset = arrived, base
            if level > 0:
                value = arrived[base + start : base + stop, :]
                if shift:
                    value = pltpu.roll(value, width - shift, 1)
                source, offset = clean[level if shift == shift_of(level) else 0], -start
                source[: stop - start, :] = jnp.where(lax.rem(lane, spacing) == 0, value, 0.0)
            held |= {plane: (source, at + offset) for plane, at in here.items()}

        def read(plane):
            source, at = held[plane]
            return source[at : at + height, :]

        def add(plane, value):
            x = (plane - to * (block >> level)) * spacing
            out[x, pl.ds(0, height, spacing), :] += value

        for plane in held:
            add(plane, read(plane))
        for (found, plane), (far, near) in derived.items():
            if found == level:
                if near is None:
                    value = (d / SCALE**2) * read(far)
                else:
                    value = ((1 / c + d) / SCALE**2) * read(far) + (d / SCALE**2) * read(near)
                row = lax.broadcasted_iota(jnp.int32, shape, 0)
                keep = (lax.rem(row, 2) == 1) | lanes_of(width, spacing, True)
                add(plane, jnp.where(keep, value, 0.0))


def write_out(out, whole, done, runs):
    copies = [
        pltpu.make_async_copy(
            out.at[pl.ds(start, stop - start)], whole.at[pl.ds(start, stop - start)], done.at[n]
        )
        for n, (start, stop) in enumerate(runs)
    ]
    for copy in copies:
        copy.start()
    for copy in copies:
        copy.wait()


def add_kernel(block, rows, places, last, _, *refs):
    received, refs = refs[: len(places)], refs[len(places) :]
    if last:
        whole, out, done, *clean = refs
    else:
        out, *clean = refs
    for to, arrived in zip(places, received):
        add_message(block, rows, to, arrived, 0, out, clean)
    if last:
        write_out(out, whole, done, [(0, block)])


def add_far(block, rows, right, arrived, base, out, clean):
    width, level = out.shape[-1], LEVELS - 1
    spacing, height, shift = 1 << level, rows >> level, shift_of(level)
    length = max(message(block, rows, to)[2] for to in (2, -2))
    lane = lax.broadcasted_iota(jnp.int32, (1, width), 1)
    value = pltpu.roll(arrived[base : base + length, :], width - shift, 1)
    value = jnp.where(lax.rem(lane, spacing) == 0, value, 0.0)
    for to, here in ((2, right), (-2, jnp.logical_not(right))):
        source = clean[0 if to > 0 else level]
        source[:length, :] = jnp.where(here, value, 0.0)
        for (found, plane), (at, _) in message(block, rows, to)[0].items():
            x = (plane - to * (block >> level)) * spacing
            out[x, pl.ds(0, height, spacing), :] += source[at : at + height, :]


def add_either(block, rows, right, step, arrived, base, out, clean):
    for side, here in ((step, right), (-step, jnp.logical_not(right))):

        @pl.when(here)
        def _():
            add_message(block, rows, side, arrived, base, out, clean)


def keep_kernel(block, rows, _, near, far, out, *clean):
    core = lax.axis_index("gy")
    add_either(block, rows, takes_right(1), 1, half_of(near, core), 0, out, clean)
    add_far(block, rows, takes_right(2), half_of(far, core), 0, out, clean)


def half_of(arrived, core):
    size = arrived.shape[0] // 2
    return arrived.at[pl.ds(pl.multiple_of(core * size, 8), size)]


def pack_kernel(near, far, packed):
    one = near.shape[0] // 2
    other = 1 - lax.axis_index("gy")
    packed[:one, :] = half_of(near, other)[...]
    packed[one:, :] = half_of(far, other)[...]


def swap_kernel(block, rows, one, own, packed, whole, out, done, *clean):
    add_either(block, rows, jnp.logical_not(takes_right(1)), 1, packed, 0, out, clean)
    add_far(block, rows, jnp.logical_not(takes_right(2)), packed, one, out, clean)
    write_out(out, whole, done, [(0, block)])


def call(body, name, outs, ins, scratch=(), aliases=None, flops=0, hbm_out=()):
    vmem, hbm = pl.BlockSpec(memory_space=pltpu.VMEM), pl.BlockSpec(memory_space=pltpu.HBM)
    f32 = jnp.float32
    shapes = [out if isinstance(out, jax.ShapeDtypeStruct) else jax.ShapeDtypeStruct(out, f32) for out in outs]
    moved = 4 * sum(int(np.prod(shape.shape)) for shape in shapes)
    return pl.pallas_call(
        body,
        out_shape=shapes,
        in_specs=[vmem] * len(ins),
        out_specs=[hbm if n in hbm_out else vmem for n in range(len(outs))],
        scratch_shapes=[pltpu.VMEM(shape, f32) if isinstance(shape, tuple) else shape for shape in scratch],
        input_output_aliases=aliases or {},
        compiler_params=pltpu.CompilerParams(vmem_limit_bytes=VMEM_BYTES),
        cost_estimate=pl.CostEstimate(flops=flops, bytes_accessed=2 * moved, transcendentals=0),
        name=name,
    )(*ins)


def local(velocity):
    block, rows, width = velocity.shape
    around, count = lax.axis_size("gx"), lax.axis_size("gy")
    shared = count == 2 and SHARED
    places = places_of(block)
    spans = windows(block)
    total = count * rows

    others = [
        lax.ppermute(velocity, "gy", [(i, (i - k) % count) for i in range(count)])
        for k in range(1, count)
    ]
    lifted = [
        (high - low + 1, total >> level, width) for level, (low, high) in enumerate(spans)
    ]
    coarse = [
        ((high // 2 - low // 2 + 1) * (total >> (level + 1)), width)
        for level, (low, high) in enumerate(spans[:-1])
    ]
    spread = (block * rows, width)
    owned = [(block >> level, rows >> level, width) for level in range(LEVELS)]
    lengths = {to: message(block, rows, to)[2] for to in places}
    one, two = max(lengths[1], lengths[-1]), max(lengths[2], lengths[-2])
    clean = [(one, width)] * LEVELS

    square = jax.ShapeDtypeStruct((2 * width, 2 * width), jnp.bfloat16)
    weights = call(matrix_kernel, "make_matrices", [square] * 2, [], flops=FIRST_FLOPS)
    (first,) = call(
        functools.partial(own_kernel, block, rows),
        "lift_own",
        [lifted[0]],
        [velocity, weights[0]],
        [spread],
    )
    if shared:
        outs, scratch = ([(many * size, width) for size in (one, two)] for many in (2, 4))
    else:
        outs, scratch = [(lengths[to], width) for to in places], []
    values = call(
        functools.partial(message_kernel, block, rows, width, count, places),
        "make_messages",
        lifted + outs,
        [first] + others + list(weights),
        [spread] + coarse + scratch,
        {0: 0},
    )
    before, messages = values[:LEVELS], values[LEVELS:]

    def rest():
        return call(
            functools.partial(rest_kernel, block, rows, width),
            "finish_own",
            [owned[0]],
            before,
            [(block >> LEVELS - 1, total >> LEVELS - 1, width)],
        )[0]

    written = [pltpu.SemaphoreType.DMA((1,))]
    if shared:
        near, far = (
            lax.ppermute(value, ("gx", "gy"), shared_pairs(step, around))
            for step, value in enumerate(messages, 1)
        )
        result = rest()
        (packed,) = call(pack_kernel, "pack_other", [(one + two, width)], [near, far])
        packed = lax.ppermute(packed, "gy", [(0, 1), (1, 0)])
        (result,) = call(
            functools.partial(keep_kernel, block, rows),
            "add_kept",
            [owned[0]],
            [result, near, far],
            clean,
            aliases={0: 0},
        )
        whole, _ = call(
            functools.partial(swap_kernel, block, rows, one),
            "add_swapped",
            [owned[0]] * 2,
            [result, packed],
            written + clean,
            aliases={0: 1},
            hbm_out=(0,),
        )
        return whole

    sent = dict(zip(places, messages))
    received = {
        to: lax.ppermute(sent[to], "gx", [(i, (i + to) % around) for i in range(around)])
        for to in sorted(places, key=lambda to: (to < 0, abs(to)))
    }
    right = [to for to in places if to > 0]
    left = [to for to in places if to < 0]
    (result,) = call(
        functools.partial(add_kernel, block, rows, right, False),
        "add_right",
        [owned[0]],
        [rest()] + [received[to] for to in right],
        clean,
        aliases={0: 0},
        flops=FIRST_FLOPS,
    )
    whole, _ = call(
        functools.partial(add_kernel, block, rows, left, True),
        "add_left",
        [owned[0]] * 2,
        [result] + [received[to] for to in left],
        written + clean,
        aliases={0: 1},
        hbm_out=(0,),
    )
    return whole


def solution(mesh):
    return jax.shard_map(
        local, mesh=mesh, in_specs=(P("gx", "gy", None),), out_specs=P("gx", "gy", None), check_vma=False
    )
```

profile of v0, /device:TPU:0, one launch (start us, length us, event | category | flops | bytes accessed | tf_op | source)
XLA Modules:
  0.0 14.6 jit_solution(8354615908477415383)
XLA Ops:
  0.0 0.0 copy-start
  0.0 0.5 %collective-permute-start = (f32[32,32,128]{2,1,0:T(8,128)}, f32[32,32,128]{2,1,0:T(8,128)S(1)}, u32[]{:S(2)}, u32[]{:S(2)}) collective-permute-start(f32[32,32,128]{2,1,0:T(8,128)} %velocity.1), channel_id=1, source_target_pairs={{0,1},{1,0},{2,3},{3,2},{4,5},{5,4},{6,7},{7,6},{8,9},{9,8},{10,11... | collective-permute-start | bytes 1572872 | tf_op jit(solution)/shard_map/ppermute | solution.py:524
  0.5 1.2 %make_matrices.1 = (bf16[256,256]{1,0:T(8,128)(2,1)S(1)}, bf16[256,256]{1,0:T(8,128)(2,1)S(1)}) custom-call(), custom_call_target="tpu_custom_call" | custom-call | flops 10000000000 | bytes 1048576 | tf_op jit(solution)/shard_map/make_matrices/pallas_call | solution.py:502
  1.6 0.0 copy-done
  1.7 0.3 %lift_own.1.refs_0_ = f32[39,64,128]{2,1,0:T(8,128)S(1)} custom-call(f32[32,32,128]{2,1,0:T(8,128)S(1)} %copy-done, bf16[256,256]{1,0:T(8,128)(2,1)S(1)} %get-tuple-element.14.weights.refs_2_), custom_call_target="tpu_custom_call" | custom-call | bytes 2555904 | tf_op jit(solution)/shard_map/lift_own/pallas_call | solution.py:502
  2.0 0.2 %collective-permute-done.refs_1_ = f32[32,32,128]{2,1,0:T(8,128)S(1)} collective-permute-done((f32[32,32,128]{2,1,0:T(8,128)}, f32[32,32,128]{2,1,0:T(8,128)S(1)}, u32[]{:S(2)}, u32[]{:S(2)}) %collective-permute-start) | collective-permute-done | bytes 524320 | tf_op jit(solution)/shard_map/ppermute | solution.py:524
  2.2 1.1 %make_messages.1 = (f32[39,64,128]{2,1,0:T(8,128)S(1)}, f32[27,32,128]{2,1,0:T(8,128)S(1)}, f32[21,16,128]{2,1,0:T(8,128)S(1)}, f32[17,8,128]{2,1,0:T(8,128)S(1)...) custom-call(f32[39,64,128]{2,1,0:T(8,128)S(1)} %lift_own.1.refs_0_, ...), custom_call_target="tpu_custom_call", output_to_operand_aliasing={{0}: (0, {})} | custom-call | bytes 4186112 | tf_op jit(solution)/shard_map/make_messages/pallas_call | solution.py:502
  3.3 2.9 %collective-permute-start.1 = (f32[224,128]{1,0:T(8,128)S(1)}, f32[224,128]{1,0:T(8,128)S(1)}, u32[]{:S(2)}, u32[]{:S(2)}) collective-permute-start(f32[224,128]{1,0:T(8,128)S(1)} %get-tuple-element.20), channel_id=1, source_target_pairs={{0,2},{1,31},{2,4},{3,0},{4,6},{5,3},{6,8},{7,5},{8,10},{9,7},{10,... | collective-permute-start | bytes 344072 | tf_op jit(solution)/shard_map/ppermute | solution.py:575
  6.2 4.0 %collective-permute-start.2 = (f32[32,128]{1,0:T(8,128)S(1)}, f32[32,128]{1,0:T(8,128)S(1)}, u32[]{:S(2)}, u32[]{:S(2)}) collective-permute-start(f32[32,128]{1,0:T(8,128)S(1)} %get-tuple-element.21), channel_id=1, source_target_pairs={{1,4},{0,29},{2,6},{3,31},{4,8},{5,1},{6,10},{7,3},{8,12},{9,5},{1... | collective-permute-start | bytes 49160 | tf_op jit(solution)/shard_map/ppermute | solution.py:575
  10.1 2.1 %collective-permute-done.2.far = f32[32,128]{1,0:T(8,128)S(1)} collective-permute-done((f32[32,128]{1,0:T(8,128)S(1)}, f32[32,128]{1,0:T(8,128)S(1)}, u32[]{:S(2)}, u32[]{:S(2)}) %collective-permute-start.2) | collective-permute-done | bytes 16416 | tf_op jit(solution)/shard_map/ppermute | solution.py:575
  12.2 0.0 collective-permute-done.1.near
  12.2 0.5 %collective-permute-start.3 = (f32[128,128]{1,0:T(8,128)S(1)}, f32[128,128]{1,0:T(8,128)S(1)}, u32[]{:S(2)}, u32[]{:S(2)}) collective-permute-start(f32[128,128]{1,0:T(8,128)S(1)} %pack_other.1), channel_id=1, source_target_pairs={{0,1},{1,0},{2,3},{3,2},{4,5},{5,4},{6,7},{7,6},{8,9},{9,8},{10,11... | collective-permute-start | bytes 196616 | tf_op jit(solution)/shard_map/ppermute | solution.py:580
  12.7 0.4 %finish_own.1._ = f32[32,32,128]{2,1,0:T(8,128)S(1)} custom-call(f32[39,64,128]{2,1,0:T(8,128)S(1)} %get-tuple-element.16.refs_0_, f32[27,32,128]{2,1,0:T(8,128)S(1)} %get-tuple-element.17.refs_1_, f32[21,16,128]{2,1,0:T(8,128)S(1)} %get-tuple-element.18.refs_2_, f32[17,8,128]{2,1,0:T(8,128)S(1)} %get-tuple-element.19.refs_3_), custom_call_target="tpu_custom_call" | custom-call | bytes 1048576 | tf_op jit(solution)/shard_map/finish_own/pallas_call | solution.py:502
  13.1 0.2 %add_kept.1.own = f32[32,32,128]{2,1,0:T(8,128)S(1)} custom-call(f32[32,32,128]{2,1,0:T(8,128)S(1)} %finish_own.1._, f32[224,128]{1,0:T(8,128)S(1)} %collective-permute-done.1.near, f32[32,128]{1,0:T(8,128)S(1)} %collective-permute-done.2.far), custom_call_target="tpu_custom_call", output_to_operand_aliasing={{}: (0, {})} | custom-call | bytes 1048576 | tf_op jit(solution)/shard_map/add_kept/pallas_call | solution.py:502
  13.3 0.3 %collective-permute-done.3.packed = f32[128,128]{1,0:T(8,128)S(1)} collective-permute-done((f32[128,128]{1,0:T(8,128)S(1)}, f32[128,128]{1,0:T(8,128)S(1)}, u32[]{:S(2)}, u32[]{:S(2)}) %collective-permute-start.3) | collective-permute-done | bytes 65568 | tf_op jit(solution)/shard_map/ppermute | solution.py:580
  13.6 1.0 %add_swapped.1 = (f32[32,32,128]{2,1,0:T(8,128)}, f32[32,32,128]{2,1,0:T(8,128)S(1)}) custom-call(f32[32,32,128]{2,1,0:T(8,128)S(1)} %add_kept.1.own, f32[128,128]{1,0:T(8,128)S(1)} %collective-permute-done.3.packed), custom_call_target="tpu_custom_call", output_to_operand_aliasing={{1}: (0, {})} | custom-call | bytes 2097152 | tf_op jit(solution)/shard_map/add_swapped/pallas_call | solution.py:502
  (1 shorter events, 0.0 us)
Async XLA Ops:
  0.0 1.6 %copy-start = (f32[32,32,128]{2,1,0:T(8,128)S(1)}, f32[32,32,128]{2,1,0:T(8,128)}, u32[]{:S(2)}) copy-start(f32[32,32,128]{2,1,0:T(8,128)} %velocity.1) | copy-start | bytes 1572868
  0.0 2.2 %collective-permute-start = (f32[32,32,128]{2,1,0:T(8,128)}, f32[32,32,128]{2,1,0:T(8,128)S(1)}, u32[]{:S(2)}, u32[]{:S(2)}) collective-permute-start(f32[32,32,128]{2,1,0:T(8,128)} %velocity.1), channel_id=1, source_target_pairs={{0,1},{1,0},{2,3},{3,2},{4,5},{5,4},{6,7},{7,6},{8,9},{9,8},{10,11... | collective-permute-start | bytes 1572872 | tf_op jit(solution)/shard_map/ppermute | solution.py:524
  3.3 9.0 %collective-permute-start.1 = (f32[224,128]{1,0:T(8,128)S(1)}, f32[224,128]{1,0:T(8,128)S(1)}, u32[]{:S(2)}, u32[]{:S(2)}) collective-permute-start(f32[224,128]{1,0:T(8,128)S(1)} %get-tuple-element.20), channel_id=1, source_target_pairs={{0,2},{1,31},{2,4},{3,0},{4,6},{5,3},{6,8},{7,5},{8,10},{9,7},{10,... | collective-permute-start | bytes 344072 | tf_op jit(solution)/shard_map/ppermute | solution.py:575
  6.2 6.0 %collective-permute-start.2 = (f32[32,128]{1,0:T(8,128)S(1)}, f32[32,128]{1,0:T(8,128)S(1)}, u32[]{:S(2)}, u32[]{:S(2)}) collective-permute-start(f32[32,128]{1,0:T(8,128)S(1)} %get-tuple-element.21), channel_id=1, source_target_pairs={{1,4},{0,29},{2,6},{3,31},{4,8},{5,1},{6,10},{7,3},{8,12},{9,5},{1... | collective-permute-start | bytes 49160 | tf_op jit(solution)/shard_map/ppermute | solution.py:575
  12.2 1.4 %collective-permute-start.3 = (f32[128,128]{1,0:T(8,128)S(1)}, f32[128,128]{1,0:T(8,128)S(1)}, u32[]{:S(2)}, u32[]{:S(2)}) collective-permute-start(f32[128,128]{1,0:T(8,128)S(1)} %pack_other.1), channel_id=1, source_target_pairs={{0,1},{1,0},{2,3},{3,2},{4,5},{5,4},{6,7},{7,6},{8,9},{9,8},{10,11... | collective-permute-start | bytes 196616 | tf_op jit(solution)/shard_map/ppermute | solution.py:580
where the time goes:
time: 14.7 us; the launch traced here: 14.6 us
  starting transfers between devices  7.8 us (53%)
  Pallas kernels  4.18 us (28%)
  waiting for transfers between devices  2.55 us (17%)
    ppermute x2, starting transfers between devices, local(): lax.ppermute(value, ('gx', 'gy'), shared_pairs(step, around))  6.87 us
    pallas_call x7, Pallas kernels, call(): pl.pallas_call(body, out_shape=shapes, in_specs=[vmem] * len(ins), out_sp...  4.18 us
    ppermute x2, waiting for transfers between devices, local(): lax.ppermute(value, ('gx', 'gy'), shared_pairs(step, around))  2.08 us
    ppermute x1, starting transfers between devices, local(): packed = lax.ppermute(packed, 'gy', [(0, 1), (1, 0)])  0.47 us
    ppermute x1, starting transfers between devices, local(): lax.ppermute(velocity, 'gy', [(i, (i - k) % count) for i in range(count)])  0.45 us
  transfers between devices with their start and end apart: 4, of which 3 were waited for; matrix products, arithmetic and copies ran while one was open for 0% of the time, Pallas kernels for 15%

commit v1 on v0

--- a/solution.py
+++ b/solution.py
@@ -378,11 +378,12 @@
             out[x, pl.ds(spacing, mine, 2 * spacing), :] += odd
 
 
-def add_message(block, rows, to, arrived, base, out, clean):
+def additions(block, rows, to, arrived, base, out, clean):
     sent, derived, _ = message(block, rows, to)
     a, b, c, d = STEPS
     width = out.shape[-1]
     lane = lax.broadcasted_iota(jnp.int32, (1, width), 1)
+    found_here = []
     for level in sorted({level for level, _ in sent}):
         spacing, height = 1 << level, rows >> level
         shape = (height, width)
@@ -401,38 +402,44 @@
                 source[: stop - start, :] = jnp.where(lax.rem(lane, spacing) == 0, value, 0.0)
             held |= {plane: (source, at + offset) for plane, at in here.items()}
 
-        def read(plane):
+        def read(plane, held=held, height=height):
             source, at = held[plane]
             return source[at : at + height, :]
 
-        def add(plane, value):
-            x = (plane - to * (block >> level)) * spacing
-            out[x, pl.ds(0, height, spacing), :] += value
-
-        for plane in held:
-            add(plane, read(plane))
+        def derive(far, near, read=read, shape=shape, spacing=spacing):
+            if near is None:
+                value = (d / SCALE**2) * read(far)
+            else:
+                value = ((1 / c + d) / SCALE**2) * read(far) + (d / SCALE**2) * read(near)
+            row = lax.broadcasted_iota(jnp.int32, shape, 0)
+            keep = (lax.rem(row, 2) == 1) | lanes_of(width, spacing, True)
+            return jnp.where(keep, value, 0.0)
+
+        values = {plane: functools.partial(read, plane) for plane in held}
         for (found, plane), (far, near) in derived.items():
             if found == level:
-                if near is None:
-                    value = (d / SCALE**2) * read(far)
-                else:
-                    value = ((1 / c + d) / SCALE**2) * read(far) + (d / SCALE**2) * read(near)
-                row = lax.broadcasted_iota(jnp.int32, shape, 0)
-                keep = (lax.rem(row, 2) == 1) | lanes_of(width, spacing, True)
-                add(plane, jnp.where(keep, value, 0.0))
-
-
-def write_out(out, whole, done, runs):
-    copies = [
-        pltpu.make_async_copy(
-            out.at[pl.ds(start, stop - start)], whole.at[pl.ds(start, stop - start)], done.at[n]
-        )
-        for n, (start, stop) in enumerate(runs)
-    ]
-    for copy in copies:
-        copy.start()
-    for copy in copies:
-        copy.wait()
+                values[plane] = functools.partial(derive, far, near)
+        for plane, value in values.items():
+            x = (plane - to * (block >> level)) * spacing
+
+            def add(x=x, height=height, spacing=spacing, value=value):
+                out[x, pl.ds(0, height, spacing), :] += value()
+
+            found_here.append((x, add))
+    return found_here
+
+
+def add_message(*args):
+    for _, add in additions(*args):
+        add()
+
+
+def copy_out(out, whole, done, part, parts):
+    size = out.shape[0] // parts
+    here = pl.ds(part * size, size)
+    copy = pltpu.make_async_copy(out.at[here], whole.at[here], done.at[part])
+    copy.start()
+    return copy
 
 
 def add_kernel(block, rows, places, last, _, *refs):
@@ -444,7 +451,8 @@
     for to, arrived in zip(places, received):
         add_message(block, rows, to, arrived, 0, out, clean)
     if last:
-        write_out(out, whole, done, [(0, block)])
+        for copy in [copy_out(out, whole, done, part, 2) for part in range(2)]:
+            copy.wait()
 
 
 def add_far(block, rows, right, arrived, base, out, clean):
@@ -489,9 +497,21 @@
 
 
 def swap_kernel(block, rows, one, own, packed, whole, out, done, *clean):
-    add_either(block, rows, jnp.logical_not(takes_right(1)), 1, packed, 0, out, clean)
     add_far(block, rows, jnp.logical_not(takes_right(2)), packed, one, out, clean)
-    write_out(out, whole, done, [(0, block)])
+    right = jnp.logical_not(takes_right(1))
+    for to, here in ((1, right), (-1, jnp.logical_not(right))):
+
+        @pl.when(here)
+        def _():
+            tasks = additions(block, rows, to, packed, 0, out, clean)
+            copies = []
+            for part in ((1, 0) if to > 0 else (0, 1)):
+                for x, add in tasks:
+                    if 2 * x // block == part:
+                        add()
+                copies.append(copy_out(out, whole, done, part, 2))
+            for copy in copies:
+                copy.wait()
 
 
 def call(body, name, outs, ins, scratch=(), aliases=None, flops=0, hbm_out=()):
@@ -569,7 +589,7 @@
             [(block >> LEVELS - 1, total >> LEVELS - 1, width)],
         )[0]
 
-    written = [pltpu.SemaphoreType.DMA((1,))]
+    written = [pltpu.SemaphoreType.DMA((2,))]
     if shared:
         near, far = (
             lax.ppermute(value, ("gx", "gy"), shared_pairs(step, around))

time: 14.7 us -> 14.7 us (level)
  no operation moved by 1% of the time
where the time goes in v1:
time: 14.7 us; the launch traced here: 14.5 us
  starting transfers between devices  7.8 us (53%)
  Pallas kernels  4.12 us (28%)
  waiting for transfers between devices  2.55 us (17%)
    ppermute x2, starting transfers between devices, local(): lax.ppermute(value, ('gx', 'gy'), shared_pairs(step, around))  6.87 us
    pallas_call x7, Pallas kernels, call(): pl.pallas_call(body, out_shape=shapes, in_specs=[vmem] * len(ins), out_sp...  4.12 us
    ppermute x2, waiting for transfers between devices, local(): lax.ppermute(value, ('gx', 'gy'), shared_pairs(step, around))  2.08 us
    ppermute x1, starting transfers between devices, local(): packed = lax.ppermute(packed, 'gy', [(0, 1), (1, 0)])  0.47 us
    ppermute x1, starting transfers between devices, local(): lax.ppermute(velocity, 'gy', [(i, (i - k) % count) for i in range(count)])  0.45 us
  transfers between devices with their start and end apart: 4, of which 3 were waited for; matrix products, arithmetic and copies ran while one was open for 0% of the time, Pallas kernels for 15%

profile of v1, /device:TPU:0, one launch (start us, length us, event | category | flops | bytes accessed | tf_op | source)
XLA Modules:
  0.0 14.5 jit_solution(7969775076738411333)
XLA Ops:
  0.0 0.0 copy-start
  0.0 0.5 %collective-permute-start = (f32[32,32,128]{2,1,0:T(8,128)}, f32[32,32,128]{2,1,0:T(8,128)S(1)}, u32[]{:S(2)}, u32[]{:S(2)}) collective-permute-start(f32[32,32,128]{2,1,0:T(8,128)} %velocity.1), channel_id=1, source_target_pairs={{0,1},{1,0},{2,3},{3,2},{4,5},{5,4},{6,7},{7,6},{8,9},{9,8},{10,11... | collective-permute-start | bytes 1572872 | tf_op jit(solution)/shard_map/ppermute | solution.py:544
  0.5 1.2 %make_matrices.1 = (bf16[256,256]{1,0:T(8,128)(2,1)S(1)}, bf16[256,256]{1,0:T(8,128)(2,1)S(1)}) custom-call(), custom_call_target="tpu_custom_call" | custom-call | flops 10000000000 | bytes 1048576 | tf_op jit(solution)/shard_map/make_matrices/pallas_call | solution.py:522
  1.6 0.0 copy-done
  1.7 0.3 %lift_own.1.refs_0_ = f32[39,64,128]{2,1,0:T(8,128)S(1)} custom-call(f32[32,32,128]{2,1,0:T(8,128)S(1)} %copy-done, bf16[256,256]{1,0:T(8,128)(2,1)S(1)} %get-tuple-element.14.weights.refs_2_), custom_call_target="tpu_custom_call" | custom-call | bytes 2555904 | tf_op jit(solution)/shard_map/lift_own/pallas_call | solution.py:522
  2.0 0.2 %collective-permute-done.refs_1_ = f32[32,32,128]{2,1,0:T(8,128)S(1)} collective-permute-done((f32[32,32,128]{2,1,0:T(8,128)}, f32[32,32,128]{2,1,0:T(8,128)S(1)}, u32[]{:S(2)}, u32[]{:S(2)}) %collective-permute-start) | collective-permute-done | bytes 524320 | tf_op jit(solution)/shard_map/ppermute | solution.py:544
  2.2 1.1 %make_messages.1 = (f32[39,64,128]{2,1,0:T(8,128)S(1)}, f32[27,32,128]{2,1,0:T(8,128)S(1)}, f32[21,16,128]{2,1,0:T(8,128)S(1)}, f32[17,8,128]{2,1,0:T(8,128)S(1)...) custom-call(f32[39,64,128]{2,1,0:T(8,128)S(1)} %lift_own.1.refs_0_, ...), custom_call_target="tpu_custom_call", output_to_operand_aliasing={{0}: (0, {})} | custom-call | bytes 4186112 | tf_op jit(solution)/shard_map/make_messages/pallas_call | solution.py:522
  3.3 2.9 %collective-permute-start.1 = (f32[224,128]{1,0:T(8,128)S(1)}, f32[224,128]{1,0:T(8,128)S(1)}, u32[]{:S(2)}, u32[]{:S(2)}) collective-permute-start(f32[224,128]{1,0:T(8,128)S(1)} %get-tuple-element.20), channel_id=1, source_target_pairs={{0,2},{1,31},{2,4},{3,0},{4,6},{5,3},{6,8},{7,5},{8,10},{9,7},{10,... | collective-permute-start | bytes 344072 | tf_op jit(solution)/shard_map/ppermute | solution.py:595
  6.2 4.0 %collective-permute-start.2 = (f32[32,128]{1,0:T(8,128)S(1)}, f32[32,128]{1,0:T(8,128)S(1)}, u32[]{:S(2)}, u32[]{:S(2)}) collective-permute-start(f32[32,128]{1,0:T(8,128)S(1)} %get-tuple-element.21), channel_id=1, source_target_pairs={{1,4},{0,29},{2,6},{3,31},{4,8},{5,1},{6,10},{7,3},{8,12},{9,5},{1... | collective-permute-start | bytes 49160 | tf_op jit(solution)/shard_map/ppermute | solution.py:595
  10.1 2.1 %collective-permute-done.2.far = f32[32,128]{1,0:T(8,128)S(1)} collective-permute-done((f32[32,128]{1,0:T(8,128)S(1)}, f32[32,128]{1,0:T(8,128)S(1)}, u32[]{:S(2)}, u32[]{:S(2)}) %collective-permute-start.2) | collective-permute-done | bytes 16416 | tf_op jit(solution)/shard_map/ppermute | solution.py:595
  12.2 0.0 collective-permute-done.1.near
  12.2 0.5 %collective-permute-start.3 = (f32[128,128]{1,0:T(8,128)S(1)}, f32[128,128]{1,0:T(8,128)S(1)}, u32[]{:S(2)}, u32[]{:S(2)}) collective-permute-start(f32[128,128]{1,0:T(8,128)S(1)} %pack_other.1), channel_id=1, source_target_pairs={{0,1},{1,0},{2,3},{3,2},{4,5},{5,4},{6,7},{7,6},{8,9},{9,8},{10,11... | collective-permute-start | bytes 196616 | tf_op jit(solution)/shard_map/ppermute | solution.py:600
  12.7 0.4 %finish_own.1._ = f32[32,32,128]{2,1,0:T(8,128)S(1)} custom-call(f32[39,64,128]{2,1,0:T(8,128)S(1)} %get-tuple-element.16.refs_0_, f32[27,32,128]{2,1,0:T(8,128)S(1)} %get-tuple-element.17.refs_1_, f32[21,16,128]{2,1,0:T(8,128)S(1)} %get-tuple-element.18.refs_2_, f32[17,8,128]{2,1,0:T(8,128)S(1)} %get-tuple-element.19.refs_3_), custom_call_target="tpu_custom_call" | custom-call | bytes 1048576 | tf_op jit(solution)/shard_map/finish_own/pallas_call | solution.py:522
  13.1 0.2 %add_kept.1.own = f32[32,32,128]{2,1,0:T(8,128)S(1)} custom-call(f32[32,32,128]{2,1,0:T(8,128)S(1)} %finish_own.1._, f32[224,128]{1,0:T(8,128)S(1)} %collective-permute-done.1.near, f32[32,128]{1,0:T(8,128)S(1)} %collective-permute-done.2.far), custom_call_target="tpu_custom_call", output_to_operand_aliasing={{}: (0, {})} | custom-call | bytes 1048576 | tf_op jit(solution)/shard_map/add_kept/pallas_call | solution.py:522
  13.3 0.3 %collective-permute-done.3.packed = f32[128,128]{1,0:T(8,128)S(1)} collective-permute-done((f32[128,128]{1,0:T(8,128)S(1)}, f32[128,128]{1,0:T(8,128)S(1)}, u32[]{:S(2)}, u32[]{:S(2)}) %collective-permute-start.3) | collective-permute-done | bytes 65568 | tf_op jit(solution)/shard_map/ppermute | solution.py:600
  13.6 0.9 %add_swapped.1 = (f32[32,32,128]{2,1,0:T(8,128)}, f32[32,32,128]{2,1,0:T(8,128)S(1)}) custom-call(f32[32,32,128]{2,1,0:T(8,128)S(1)} %add_kept.1.own, f32[128,128]{1,0:T(8,128)S(1)} %collective-permute-done.3.packed), custom_call_target="tpu_custom_call", output_to_operand_aliasing={{1}: (0, {})} | custom-call | bytes 2097152 | tf_op jit(solution)/shard_map/add_swapped/pallas_call | solution.py:522
  (1 shorter events, 0.0 us)
Async XLA Ops:
  0.0 1.6 %copy-start = (f32[32,32,128]{2,1,0:T(8,128)S(1)}, f32[32,32,128]{2,1,0:T(8,128)}, u32[]{:S(2)}) copy-start(f32[32,32,128]{2,1,0:T(8,128)} %velocity.1) | copy-start | bytes 1572868
  0.0 2.2 %collective-permute-start = (f32[32,32,128]{2,1,0:T(8,128)}, f32[32,32,128]{2,1,0:T(8,128)S(1)}, u32[]{:S(2)}, u32[]{:S(2)}) collective-permute-start(f32[32,32,128]{2,1,0:T(8,128)} %velocity.1), channel_id=1, source_target_pairs={{0,1},{1,0},{2,3},{3,2},{4,5},{5,4},{6,7},{7,6},{8,9},{9,8},{10,11... | collective-permute-start | bytes 1572872 | tf_op jit(solution)/shard_map/ppermute | solution.py:544
  3.3 9.0 %collective-permute-start.1 = (f32[224,128]{1,0:T(8,128)S(1)}, f32[224,128]{1,0:T(8,128)S(1)}, u32[]{:S(2)}, u32[]{:S(2)}) collective-permute-start(f32[224,128]{1,0:T(8,128)S(1)} %get-tuple-element.20), channel_id=1, source_target_pairs={{0,2},{1,31},{2,4},{3,0},{4,6},{5,3},{6,8},{7,5},{8,10},{9,7},{10,... | collective-permute-start | bytes 344072 | tf_op jit(solution)/shard_map/ppermute | solution.py:595
  6.2 6.0 %collective-permute-start.2 = (f32[32,128]{1,0:T(8,128)S(1)}, f32[32,128]{1,0:T(8,128)S(1)}, u32[]{:S(2)}, u32[]{:S(2)}) collective-permute-start(f32[32,128]{1,0:T(8,128)S(1)} %get-tuple-element.21), channel_id=1, source_target_pairs={{1,4},{0,29},{2,6},{3,31},{4,8},{5,1},{6,10},{7,3},{8,12},{9,5},{1... | collective-permute-start | bytes 49160 | tf_op jit(solution)/shard_map/ppermute | solution.py:595
  12.2 1.4 %collective-permute-start.3 = (f32[128,128]{1,0:T(8,128)S(1)}, f32[128,128]{1,0:T(8,128)S(1)}, u32[]{:S(2)}, u32[]{:S(2)}) collective-permute-start(f32[128,128]{1,0:T(8,128)S(1)} %pack_other.1), channel_id=1, source_target_pairs={{0,1},{1,0},{2,3},{3,2},{4,5},{5,4},{6,7},{7,6},{8,9},{9,8},{10,11... | collective-permute-start | bytes 196616 | tf_op jit(solution)/shard_map/ppermute | solution.py:600

commit v2 on v1

--- a/solution.py
+++ b/solution.py
@@ -73,13 +73,25 @@
     return sorted(found - {0})
 
 
+def in_parts(value):
+    parts = []
+    for _ in range(3):
+        parts.append(value.astype(jnp.bfloat16))
+        value = value - parts[-1].astype(jnp.float32)
+    return parts
+
+
 def z_product(value, weights):
     width = value.shape[-1]
-    high = value.astype(jnp.bfloat16)
-    rest = (value - high.astype(jnp.float32)).astype(jnp.bfloat16)
-    both = jnp.concatenate([high, rest], axis=1)
-    product = jnp.dot(both, weights, preferred_element_type=jnp.float32)
-    return product[:, :width] + product[:, width:]
+    high, middle, low = in_parts(value)
+
+    def dot(left, right, matrix):
+        both = jnp.concatenate([left, right], axis=1)
+        return jnp.dot(both, matrix, preferred_element_type=jnp.float32)
+
+    large = dot(high, middle, weights[:, : 2 * width])
+    small = dot(low, high, weights[:, 2 * width :])
+    return large[:, :width] + (large[:, width:] + small)
 
 
 def lanes_of(width, spacing, parity):
@@ -175,12 +187,10 @@
         full[1] += pltpu.roll(value, shift_of(level), 1) if shift_of(level) else value
         value = jnp.where(lanes_of(width, spacing, False), value, 0.0)
     for weight, matrix in zip(weights, full):
-        high = matrix.astype(jnp.bfloat16)
-        rest = (matrix - high.astype(jnp.float32)).astype(jnp.bfloat16)
-        weight[:width, :width] = high
-        weight[:width, width:] = rest
-        weight[width:, :width] = high
-        weight[width:, width:] = jnp.zeros_like(rest)
+        high, middle, low = in_parts(matrix)
+        for at, column in enumerate(((high, middle), (middle, high), (high, low))):
+            for row, part in enumerate(column):
+                weight[row * width : (row + 1) * width, at * width : (at + 1) * width] = part
 
 
 def own_kernel(block, rows, velocity, weights, into, spread):
@@ -557,7 +567,7 @@
     one, two = max(lengths[1], lengths[-1]), max(lengths[2], lengths[-2])
     clean = [(one, width)] * LEVELS
 
-    square = jax.ShapeDtypeStruct((2 * width, 2 * width), jnp.bfloat16)
+    square = jax.ShapeDtypeStruct((2 * width, 3 * width), jnp.bfloat16)
     weights = call(matrix_kernel, "make_matrices", [square] * 2, [], flops=FIRST_FLOPS)
     (first,) = call(
         functools.partial(own_kernel, block, rows),

time: 14.7 us -> 14.8 us (level)
  Pallas kernels: 4.12 us -> 4.35 us
    pallas_call x7, Pallas kernels: 4.12 us -> 4.35 us  [call(): pl.pallas_call(body, out_shape=shapes, in_specs=[vmem] * len(ins), out_sp...]
  transfers between devices with their start and end apart: 4 -> 4, of which waited for: 3 -> 3; matrix products, arithmetic and copies ran while one was open for 0% -> 0% of each run, Pallas kernels for 15% -> 16%
where the time goes in v2:
time: 14.8 us; the launch traced here: 14.6 us
  starting transfers between devices  7.8 us (53%)
  Pallas kernels  4.35 us (29%)
  waiting for transfers between devices  2.42 us (16%)
    ppermute x2, starting transfers between devices, local(): lax.ppermute(value, ('gx', 'gy'), shared_pairs(step, around))  6.87 us
    pallas_call x7, Pallas kernels, call(): pl.pallas_call(body, out_shape=shapes, in_specs=[vmem] * len(ins), out_sp...  4.35 us
    ppermute x2, waiting for transfers between devices, local(): lax.ppermute(value, ('gx', 'gy'), shared_pairs(step, around))  2.07 us
    ppermute x1, starting transfers between devices, local(): packed = lax.ppermute(packed, 'gy', [(0, 1), (1, 0)])  0.47 us
    ppermute x1, starting transfers between devices, local(): lax.ppermute(velocity, 'gy', [(i, (i - k) % count) for i in range(count)])  0.45 us
  transfers between devices with their start and end apart: 4, of which 3 were waited for; matrix products, arithmetic and copies ran while one was open for 0% of the time, Pallas kernels for 16%

profile of v2, /device:TPU:0, one launch (start us, length us, event | category | flops | bytes accessed | tf_op | source)
XLA Modules:
  0.0 14.6 jit_solution(5268498730896378170)
XLA Ops:
  0.0 0.0 copy-start
  0.0 0.5 %collective-permute-start = (f32[32,32,128]{2,1,0:T(8,128)}, f32[32,32,128]{2,1,0:T(8,128)S(1)}, u32[]{:S(2)}, u32[]{:S(2)}) collective-permute-start(f32[32,32,128]{2,1,0:T(8,128)} %velocity.1), channel_id=1, source_target_pairs={{0,1},{1,0},{2,3},{3,2},{4,5},{5,4},{6,7},{7,6},{8,9},{9,8},{10,11... | collective-permute-start | bytes 1572872 | tf_op jit(solution)/shard_map/ppermute | solution.py:554
  0.5 1.2 %make_matrices.1 = (bf16[256,384]{1,0:T(8,128)(2,1)S(1)}, bf16[256,384]{1,0:T(8,128)(2,1)S(1)}) custom-call(), custom_call_target="tpu_custom_call" | custom-call | flops 10000000000 | bytes 1572864 | tf_op jit(solution)/shard_map/make_matrices/pallas_call | solution.py:532
  1.7 0.0 copy-done
  1.7 0.5 %lift_own.1.refs_0_ = f32[39,64,128]{2,1,0:T(8,128)S(1)} custom-call(f32[32,32,128]{2,1,0:T(8,128)S(1)} %copy-done, bf16[256,384]{1,0:T(8,128)(2,1)S(1)} %get-tuple-element.14.weights.refs_2_), custom_call_target="tpu_custom_call" | custom-call | bytes 2555904 | tf_op jit(solution)/shard_map/lift_own/pallas_call | solution.py:532
  2.1 0.1 collective-permute-done.refs_1_
  2.2 1.2 %make_messages.1 = (f32[39,64,128]{2,1,0:T(8,128)S(1)}, f32[27,32,128]{2,1,0:T(8,128)S(1)}, f32[21,16,128]{2,1,0:T(8,128)S(1)}, f32[17,8,128]{2,1,0:T(8,128)S(1)...) custom-call(f32[39,64,128]{2,1,0:T(8,128)S(1)} %lift_own.1.refs_0_, ...), custom_call_target="tpu_custom_call", output_to_operand_aliasing={{0}: (0, {})} | custom-call | bytes 4186112 | tf_op jit(solution)/shard_map/make_messages/pallas_call | solution.py:532
  3.4 2.9 %collective-permute-start.1 = (f32[224,128]{1,0:T(8,128)S(1)}, f32[224,128]{1,0:T(8,128)S(1)}, u32[]{:S(2)}, u32[]{:S(2)}) collective-permute-start(f32[224,128]{1,0:T(8,128)S(1)} %get-tuple-element.20), channel_id=1, source_target_pairs={{0,2},{1,31},{2,4},{3,0},{4,6},{5,3},{6,8},{7,5},{8,10},{9,7},{10,... | collective-permute-start | bytes 344072 | tf_op jit(solution)/shard_map/ppermute | solution.py:605
  6.3 4.0 %collective-permute-start.2 = (f32[32,128]{1,0:T(8,128)S(1)}, f32[32,128]{1,0:T(8,128)S(1)}, u32[]{:S(2)}, u32[]{:S(2)}) collective-permute-start(f32[32,128]{1,0:T(8,128)S(1)} %get-tuple-element.21), channel_id=1, source_target_pairs={{1,4},{0,29},{2,6},{3,31},{4,8},{5,1},{6,10},{7,3},{8,12},{9,5},{1... | collective-permute-start | bytes 49160 | tf_op jit(solution)/shard_map/ppermute | solution.py:605
  10.2 2.1 %collective-permute-done.2.far = f32[32,128]{1,0:T(8,128)S(1)} collective-permute-done((f32[32,128]{1,0:T(8,128)S(1)}, f32[32,128]{1,0:T(8,128)S(1)}, u32[]{:S(2)}, u32[]{:S(2)}) %collective-permute-start.2) | collective-permute-done | bytes 16416 | tf_op jit(solution)/shard_map/ppermute | solution.py:605
  12.3 0.0 collective-permute-done.1.near
  12.3 0.5 %collective-permute-start.3 = (f32[128,128]{1,0:T(8,128)S(1)}, f32[128,128]{1,0:T(8,128)S(1)}, u32[]{:S(2)}, u32[]{:S(2)}) collective-permute-start(f32[128,128]{1,0:T(8,128)S(1)} %pack_other.1), channel_id=1, source_target_pairs={{0,1},{1,0},{2,3},{3,2},{4,5},{5,4},{6,7},{7,6},{8,9},{9,8},{10,11... | collective-permute-start | bytes 196616 | tf_op jit(solution)/shard_map/ppermute | solution.py:610
  12.8 0.4 %finish_own.1._ = f32[32,32,128]{2,1,0:T(8,128)S(1)} custom-call(f32[39,64,128]{2,1,0:T(8,128)S(1)} %get-tuple-element.16.refs_0_, f32[27,32,128]{2,1,0:T(8,128)S(1)} %get-tuple-element.17.refs_1_, f32[21,16,128]{2,1,0:T(8,128)S(1)} %get-tuple-element.18.refs_2_, f32[17,8,128]{2,1,0:T(8,128)S(1)} %get-tuple-element.19.refs_3_), custom_call_target="tpu_custom_call" | custom-call | bytes 1048576 | tf_op jit(solution)/shard_map/finish_own/pallas_call | solution.py:532
  13.2 0.2 %add_kept.1.own = f32[32,32,128]{2,1,0:T(8,128)S(1)} custom-call(f32[32,32,128]{2,1,0:T(8,128)S(1)} %finish_own.1._, f32[224,128]{1,0:T(8,128)S(1)} %collective-permute-done.1.near, f32[32,128]{1,0:T(8,128)S(1)} %collective-permute-done.2.far), custom_call_target="tpu_custom_call", output_to_operand_aliasing={{}: (0, {})} | custom-call | bytes 1048576 | tf_op jit(solution)/shard_map/add_kept/pallas_call | solution.py:532
  13.4 0.3 %collective-permute-done.3.packed = f32[128,128]{1,0:T(8,128)S(1)} collective-permute-done((f32[128,128]{1,0:T(8,128)S(1)}, f32[128,128]{1,0:T(8,128)S(1)}, u32[]{:S(2)}, u32[]{:S(2)}) %collective-permute-start.3) | collective-permute-done | bytes 65568 | tf_op jit(solution)/shard_map/ppermute | solution.py:610
  13.7 0.9 %add_swapped.1 = (f32[32,32,128]{2,1,0:T(8,128)}, f32[32,32,128]{2,1,0:T(8,128)S(1)}) custom-call(f32[32,32,128]{2,1,0:T(8,128)S(1)} %add_kept.1.own, f32[128,128]{1,0:T(8,128)S(1)} %collective-permute-done.3.packed), custom_call_target="tpu_custom_call", output_to_operand_aliasing={{1}: (0, {})} | custom-call | bytes 2097152 | tf_op jit(solution)/shard_map/add_swapped/pallas_call | solution.py:532
  (1 shorter events, 0.0 us)
Async XLA Ops:
  0.0 1.7 %copy-start = (f32[32,32,128]{2,1,0:T(8,128)S(1)}, f32[32,32,128]{2,1,0:T(8,128)}, u32[]{:S(2)}) copy-start(f32[32,32,128]{2,1,0:T(8,128)} %velocity.1) | copy-start | bytes 1572868
  0.0 2.2 %collective-permute-start = (f32[32,32,128]{2,1,0:T(8,128)}, f32[32,32,128]{2,1,0:T(8,128)S(1)}, u32[]{:S(2)}, u32[]{:S(2)}) collective-permute-start(f32[32,32,128]{2,1,0:T(8,128)} %velocity.1), channel_id=1, source_target_pairs={{0,1},{1,0},{2,3},{3,2},{4,5},{5,4},{6,7},{7,6},{8,9},{9,8},{10,11... | collective-permute-start | bytes 1572872 | tf_op jit(solution)/shard_map/ppermute | solution.py:554
  3.4 8.9 %collective-permute-start.1 = (f32[224,128]{1,0:T(8,128)S(1)}, f32[224,128]{1,0:T(8,128)S(1)}, u32[]{:S(2)}, u32[]{:S(2)}) collective-permute-start(f32[224,128]{1,0:T(8,128)S(1)} %get-tuple-element.20), channel_id=1, source_target_pairs={{0,2},{1,31},{2,4},{3,0},{4,6},{5,3},{6,8},{7,5},{8,10},{9,7},{10,... | collective-permute-start | bytes 344072 | tf_op jit(solution)/shard_map/ppermute | solution.py:605
  6.3 6.0 %collective-permute-start.2 = (f32[32,128]{1,0:T(8,128)S(1)}, f32[32,128]{1,0:T(8,128)S(1)}, u32[]{:S(2)}, u32[]{:S(2)}) collective-permute-start(f32[32,128]{1,0:T(8,128)S(1)} %get-tuple-element.21), channel_id=1, source_target_pairs={{1,4},{0,29},{2,6},{3,31},{4,8},{5,1},{6,10},{7,3},{8,12},{9,5},{1... | collective-permute-start | bytes 49160 | tf_op jit(solution)/shard_map/ppermute | solution.py:605
  12.3 1.4 %collective-permute-start.3 = (f32[128,128]{1,0:T(8,128)S(1)}, f32[128,128]{1,0:T(8,128)S(1)}, u32[]{:S(2)}, u32[]{:S(2)}) collective-permute-start(f32[128,128]{1,0:T(8,128)S(1)} %pack_other.1), channel_id=1, source_target_pairs={{0,1},{1,0},{2,3},{3,2},{4,5},{5,4},{6,7},{7,6},{8,9},{9,8},{10,11... | collective-permute-start | bytes 196616 | tf_op jit(solution)/shard_map/ppermute | solution.py:610

commit v3 on v2

--- a/solution.py
+++ b/solution.py
@@ -13,6 +13,7 @@
 SCALE = 1.149604398
 VMEM_BYTES = 24 * 2**20
 FIRST_FLOPS = 10**10
+PIECE = 1024
 SHARED = True
 
 
@@ -194,7 +195,7 @@
 
 
 def own_kernel(block, rows, velocity, weights, into, spread):
-    step = max(1, min(block, 512 // rows))
+    step = max(1, min(block, PIECE // rows))
     for x in range(0, block, step):
         spread_z(velocity, weights, spread, rows, x, step)
     spread_x(block, rows, spread, into, windows(block)[0][0], 0)
@@ -290,7 +291,7 @@
 
         if level == 0:
             for part, source in enumerate(others):
-                step = min(block, max(1, 512 // rows))
+                step = min(block, max(1, PIECE // rows))
                 for x in range(0, block, step):
                     spread_z(source, weights[0], spread, rows, x, step)
                 spread_x(block, rows, spread, into, low, (part + 1) * rows)
@@ -299,8 +300,8 @@
             source = coarse[level - 1]
             if level == 1:
                 size = (stop - start) * height
-                for at in range(0, size, 512):
-                    end = min(size, at + 512)
+                for at in range(0, size, PIECE):
+                    end = min(size, at + PIECE)
                     source[at:end, :] = z_product(source[at:end, :], weights[level][...])
             for at in range(0, height, 8):
                 planes = {}

time: 14.8 us -> 14.8 us (level)
  no operation moved by 1% of the time
where the time goes in v3:
time: 14.8 us; the launch traced here: 14.6 us
  starting transfers between devices  7.79 us (53%)
  Pallas kernels  4.34 us (29%)
  waiting for transfers between devices  2.43 us (16%)
    ppermute x2, starting transfers between devices, local(): lax.ppermute(value, ('gx', 'gy'), shared_pairs(step, around))  6.87 us
    pallas_call x7, Pallas kernels, call(): pl.pallas_call(body, out_shape=shapes, in_specs=[vmem] * len(ins), out_sp...  4.34 us
    ppermute x2, waiting for transfers between devices, local(): lax.ppermute(value, ('gx', 'gy'), shared_pairs(step, around))  2.08 us
    ppermute x1, starting transfers between devices, local(): packed = lax.ppermute(packed, 'gy', [(0, 1), (1, 0)])  0.47 us
    ppermute x1, starting transfers between devices, local(): lax.ppermute(velocity, 'gy', [(i, (i - k) % count) for i in range(count)])  0.45 us
  transfers between devices with their start and end apart: 4, of which 3 were waited for; matrix products, arithmetic and copies ran while one was open for 0% of the time, Pallas kernels for 16%

profile of v3, /device:TPU:0, one launch (start us, length us, event | category | flops | bytes accessed | tf_op | source)
XLA Modules:
  0.0 14.6 jit_solution(926058048230897780)
XLA Ops:
  0.0 0.0 copy-start
  0.0 0.5 %collective-permute-start = (f32[32,32,128]{2,1,0:T(8,128)}, f32[32,32,128]{2,1,0:T(8,128)S(1)}, u32[]{:S(2)}, u32[]{:S(2)}) collective-permute-start(f32[32,32,128]{2,1,0:T(8,128)} %velocity.1), channel_id=1, source_target_pairs={{0,1},{1,0},{2,3},{3,2},{4,5},{5,4},{6,7},{7,6},{8,9},{9,8},{10,11... | collective-permute-start | bytes 1572872 | tf_op jit(solution)/shard_map/ppermute | solution.py:555
  0.5 1.2 %make_matrices.1 = (bf16[256,384]{1,0:T(8,128)(2,1)S(1)}, bf16[256,384]{1,0:T(8,128)(2,1)S(1)}) custom-call(), custom_call_target="tpu_custom_call" | custom-call | flops 10000000000 | bytes 1572864 | tf_op jit(solution)/shard_map/make_matrices/pallas_call | solution.py:533
  1.7 0.0 copy-done
  1.7 0.5 %lift_own.1.refs_0_ = f32[39,64,128]{2,1,0:T(8,128)S(1)} custom-call(f32[32,32,128]{2,1,0:T(8,128)S(1)} %copy-done, bf16[256,384]{1,0:T(8,128)(2,1)S(1)} %get-tuple-element.14.weights.refs_2_), custom_call_target="tpu_custom_call" | custom-call | bytes 2555904 | tf_op jit(solution)/shard_map/lift_own/pallas_call | solution.py:533
  2.1 0.1 collective-permute-done.refs_1_
  2.2 1.2 %make_messages.1 = (f32[39,64,128]{2,1,0:T(8,128)S(1)}, f32[27,32,128]{2,1,0:T(8,128)S(1)}, f32[21,16,128]{2,1,0:T(8,128)S(1)}, f32[17,8,128]{2,1,0:T(8,128)S(1)...) custom-call(f32[39,64,128]{2,1,0:T(8,128)S(1)} %lift_own.1.refs_0_, ...), custom_call_target="tpu_custom_call", output_to_operand_aliasing={{0}: (0, {})} | custom-call | bytes 4186112 | tf_op jit(solution)/shard_map/make_messages/pallas_call | solution.py:533
  3.4 2.9 %collective-permute-start.1 = (f32[224,128]{1,0:T(8,128)S(1)}, f32[224,128]{1,0:T(8,128)S(1)}, u32[]{:S(2)}, u32[]{:S(2)}) collective-permute-start(f32[224,128]{1,0:T(8,128)S(1)} %get-tuple-element.20), channel_id=1, source_target_pairs={{0,2},{1,31},{2,4},{3,0},{4,6},{5,3},{6,8},{7,5},{8,10},{9,7},{10,... | collective-permute-start | bytes 344072 | tf_op jit(solution)/shard_map/ppermute | solution.py:606
  6.3 4.0 %collective-permute-start.2 = (f32[32,128]{1,0:T(8,128)S(1)}, f32[32,128]{1,0:T(8,128)S(1)}, u32[]{:S(2)}, u32[]{:S(2)}) collective-permute-start(f32[32,128]{1,0:T(8,128)S(1)} %get-tuple-element.21), channel_id=1, source_target_pairs={{1,4},{0,29},{2,6},{3,31},{4,8},{5,1},{6,10},{7,3},{8,12},{9,5},{1... | collective-permute-start | bytes 49160 | tf_op jit(solution)/shard_map/ppermute | solution.py:606
  10.2 2.1 %collective-permute-done.2.far = f32[32,128]{1,0:T(8,128)S(1)} collective-permute-done((f32[32,128]{1,0:T(8,128)S(1)}, f32[32,128]{1,0:T(8,128)S(1)}, u32[]{:S(2)}, u32[]{:S(2)}) %collective-permute-start.2) | collective-permute-done | bytes 16416 | tf_op jit(solution)/shard_map/ppermute | solution.py:606
  12.3 0.0 collective-permute-done.1.near
  12.3 0.5 %collective-permute-start.3 = (f32[128,128]{1,0:T(8,128)S(1)}, f32[128,128]{1,0:T(8,128)S(1)}, u32[]{:S(2)}, u32[]{:S(2)}) collective-permute-start(f32[128,128]{1,0:T(8,128)S(1)} %pack_other.1), channel_id=1, source_target_pairs={{0,1},{1,0},{2,3},{3,2},{4,5},{5,4},{6,7},{7,6},{8,9},{9,8},{10,11... | collective-permute-start | bytes 196616 | tf_op jit(solution)/shard_map/ppermute | solution.py:611
  12.8 0.4 %finish_own.1._ = f32[32,32,128]{2,1,0:T(8,128)S(1)} custom-call(f32[39,64,128]{2,1,0:T(8,128)S(1)} %get-tuple-element.16.refs_0_, f32[27,32,128]{2,1,0:T(8,128)S(1)} %get-tuple-element.17.refs_1_, f32[21,16,128]{2,1,0:T(8,128)S(1)} %get-tuple-element.18.refs_2_, f32[17,8,128]{2,1,0:T(8,128)S(1)} %get-tuple-element.19.refs_3_), custom_call_target="tpu_custom_call" | custom-call | bytes 1048576 | tf_op jit(solution)/shard_map/finish_own/pallas_call | solution.py:533
  13.2 0.2 %add_kept.1.own = f32[32,32,128]{2,1,0:T(8,128)S(1)} custom-call(f32[32,32,128]{2,1,0:T(8,128)S(1)} %finish_own.1._, f32[224,128]{1,0:T(8,128)S(1)} %collective-permute-done.1.near, f32[32,128]{1,0:T(8,128)S(1)} %collective-permute-done.2.far), custom_call_target="tpu_custom_call", output_to_operand_aliasing={{}: (0, {})} | custom-call | bytes 1048576 | tf_op jit(solution)/shard_map/add_kept/pallas_call | solution.py:533
  13.4 0.3 %collective-permute-done.3.packed = f32[128,128]{1,0:T(8,128)S(1)} collective-permute-done((f32[128,128]{1,0:T(8,128)S(1)}, f32[128,128]{1,0:T(8,128)S(1)}, u32[]{:S(2)}, u32[]{:S(2)}) %collective-permute-start.3) | collective-permute-done | bytes 65568 | tf_op jit(solution)/shard_map/ppermute | solution.py:611
  13.7 0.9 %add_swapped.1 = (f32[32,32,128]{2,1,0:T(8,128)}, f32[32,32,128]{2,1,0:T(8,128)S(1)}) custom-call(f32[32,32,128]{2,1,0:T(8,128)S(1)} %add_kept.1.own, f32[128,128]{1,0:T(8,128)S(1)} %collective-permute-done.3.packed), custom_call_target="tpu_custom_call", output_to_operand_aliasing={{1}: (0, {})} | custom-call | bytes 2097152 | tf_op jit(solution)/shard_map/add_swapped/pallas_call | solution.py:533
  (1 shorter events, 0.0 us)
Async XLA Ops:
  0.0 1.7 %copy-start = (f32[32,32,128]{2,1,0:T(8,128)S(1)}, f32[32,32,128]{2,1,0:T(8,128)}, u32[]{:S(2)}) copy-start(f32[32,32,128]{2,1,0:T(8,128)} %velocity.1) | copy-start | bytes 1572868
  0.0 2.2 %collective-permute-start = (f32[32,32,128]{2,1,0:T(8,128)}, f32[32,32,128]{2,1,0:T(8,128)S(1)}, u32[]{:S(2)}, u32[]{:S(2)}) collective-permute-start(f32[32,32,128]{2,1,0:T(8,128)} %velocity.1), channel_id=1, source_target_pairs={{0,1},{1,0},{2,3},{3,2},{4,5},{5,4},{6,7},{7,6},{8,9},{9,8},{10,11... | collective-permute-start | bytes 1572872 | tf_op jit(solution)/shard_map/ppermute | solution.py:555
  3.4 9.0 %collective-permute-start.1 = (f32[224,128]{1,0:T(8,128)S(1)}, f32[224,128]{1,0:T(8,128)S(1)}, u32[]{:S(2)}, u32[]{:S(2)}) collective-permute-start(f32[224,128]{1,0:T(8,128)S(1)} %get-tuple-element.20), channel_id=1, source_target_pairs={{0,2},{1,31},{2,4},{3,0},{4,6},{5,3},{6,8},{7,5},{8,10},{9,7},{10,... | collective-permute-start | bytes 344072 | tf_op jit(solution)/shard_map/ppermute | solution.py:606
  6.3 6.0 %collective-permute-start.2 = (f32[32,128]{1,0:T(8,128)S(1)}, f32[32,128]{1,0:T(8,128)S(1)}, u32[]{:S(2)}, u32[]{:S(2)}) collective-permute-start(f32[32,128]{1,0:T(8,128)S(1)} %get-tuple-element.21), channel_id=1, source_target_pairs={{1,4},{0,29},{2,6},{3,31},{4,8},{5,1},{6,10},{7,3},{8,12},{9,5},{1... | collective-permute-start | bytes 49160 | tf_op jit(solution)/shard_map/ppermute | solution.py:606
  12.3 1.4 %collective-permute-start.3 = (f32[128,128]{1,0:T(8,128)S(1)}, f32[128,128]{1,0:T(8,128)S(1)}, u32[]{:S(2)}, u32[]{:S(2)}) collective-permute-start(f32[128,128]{1,0:T(8,128)S(1)} %pack_other.1), channel_id=1, source_target_pairs={{0,1},{1,0},{2,3},{3,2},{4,5},{5,4},{6,7},{7,6},{8,9},{9,8},{10,11... | collective-permute-start | bytes 196616 | tf_op jit(solution)/shard_map/ppermute | solution.py:611

commit v4 on v3

--- a/solution.py
+++ b/solution.py
@@ -36,8 +36,8 @@
         size, height = block >> level, rows >> level
         first, last = (0, block - 1) if level == 0 else (v // 2 for v in spans[level - 1])
         planes = [p for p in range(low, high + 1) if p // size == to]
-        if abs(to) == 1:
-            sign = to
+        if planes:
+            sign = 1 if to > 0 else -1
             edge = last + 2 - last % 2 if to > 0 else first - 2 + first % 2
             far, near = edge + sign, edge - sign
             if far in planes and edge + 2 * sign in planes:
@@ -417,11 +417,13 @@
             source, at = held[plane]
             return source[at : at + height, :]
 
-        def derive(far, near, read=read, shape=shape, spacing=spacing):
+        def derive(far, near, read=read, shape=shape, spacing=spacing, last=level == LEVELS - 1):
             if near is None:
                 value = (d / SCALE**2) * read(far)
             else:
                 value = ((1 / c + d) / SCALE**2) * read(far) + (d / SCALE**2) * read(near)
+            if last:
+                return value
             row = lax.broadcasted_iota(jnp.int32, shape, 0)
             keep = (lax.rem(row, 2) == 1) | lanes_of(width, spacing, True)
             return jnp.where(keep, value, 0.0)
@@ -476,9 +478,15 @@
     for to, here in ((2, right), (-2, jnp.logical_not(right))):
         source = clean[0 if to > 0 else level]
         source[:length, :] = jnp.where(here, value, 0.0)
-        for (found, plane), (at, _) in message(block, rows, to)[0].items():
+        sent, derived, _ = message(block, rows, to)
+        parts = [(plane, at, 1.0) for (_, plane), (at, _) in sent.items()]
+        parts += [
+            (plane, sent[level, far][0], STEPS[3] / SCALE**2) for (_, plane), (far, _) in derived.items()
+        ]
+        for plane, at, factor in parts:
             x = (plane - to * (block >> level)) * spacing
-            out[x, pl.ds(0, height, spacing), :] += source[at : at + height, :]
+            part = source[at : at + height, :]
+            out[x, pl.ds(0, height, spacing), :] += part if factor == 1.0 else factor * part
 
 
 def add_either(block, rows, right, step, arrived, base, out, clean):

time: 14.8 us -> 14.6 us (0.986)
  waiting for transfers between devices: 2.43 us -> 2.25 us
    ppermute x2, waiting for transfers between devices: 2.08 us -> 1.9 us  [local(): lax.ppermute(value, ('gx', 'gy'), shared_pairs(step, around))]
where the time goes in v4:
time: 14.6 us; the launch traced here: 14.5 us
  starting transfers between devices  7.88 us (54%)
  Pallas kernels  4.33 us (30%)
  waiting for transfers between devices  2.25 us (15%)
    ppermute x2, starting transfers between devices, local(): lax.ppermute(value, ('gx', 'gy'), shared_pairs(step, around))  6.87 us
    pallas_call x7, Pallas kernels, call(): pl.pallas_call(body, out_shape=shapes, in_specs=[vmem] * len(ins), out_sp...  4.33 us
    ppermute x2, waiting for transfers between devices, local(): lax.ppermute(value, ('gx', 'gy'), shared_pairs(step, around))  1.9 us
    ppermute x1, starting transfers between devices, local(): packed = lax.ppermute(packed, 'gy', [(0, 1), (1, 0)])  0.56 us
    ppermute x1, starting transfers between devices, local(): lax.ppermute(velocity, 'gy', [(i, (i - k) % count) for i in range(count)])  0.45 us
  transfers between devices with their start and end apart: 4, of which 3 were waited for; matrix products, arithmetic and copies ran while one was open for 0% of the time, Pallas kernels for 16%

profile of v4, /device:TPU:0, one launch (start us, length us, event | category | flops | bytes accessed | tf_op | source)
XLA Modules:
  0.0 14.5 jit_solution(15944836795990877363)
XLA Ops:
  0.0 0.0 copy-start
  0.0 0.5 %collective-permute-start = (f32[32,32,128]{2,1,0:T(8,128)}, f32[32,32,128]{2,1,0:T(8,128)S(1)}, u32[]{:S(2)}, u32[]{:S(2)}) collective-permute-start(f32[32,32,128]{2,1,0:T(8,128)} %velocity.1), channel_id=1, source_target_pairs={{0,1},{1,0},{2,3},{3,2},{4,5},{5,4},{6,7},{7,6},{8,9},{9,8},{10,11... | collective-permute-start | bytes 1572872 | tf_op jit(solution)/shard_map/ppermute | solution.py:563
  0.5 1.2 %make_matrices.1 = (bf16[256,384]{1,0:T(8,128)(2,1)S(1)}, bf16[256,384]{1,0:T(8,128)(2,1)S(1)}) custom-call(), custom_call_target="tpu_custom_call" | custom-call | flops 10000000000 | bytes 1572864 | tf_op jit(solution)/shard_map/make_matrices/pallas_call | solution.py:541
  1.7 0.0 copy-done
  1.7 0.5 %lift_own.1.refs_0_ = f32[39,64,128]{2,1,0:T(8,128)S(1)} custom-call(f32[32,32,128]{2,1,0:T(8,128)S(1)} %copy-done, bf16[256,384]{1,0:T(8,128)(2,1)S(1)} %get-tuple-element.14.weights.refs_2_), custom_call_target="tpu_custom_call" | custom-call | bytes 2555904 | tf_op jit(solution)/shard_map/lift_own/pallas_call | solution.py:541
  2.1 0.1 collective-permute-done.refs_1_
  2.2 1.1 %make_messages.1 = (f32[39,64,128]{2,1,0:T(8,128)S(1)}, f32[27,32,128]{2,1,0:T(8,128)S(1)}, f32[21,16,128]{2,1,0:T(8,128)S(1)}, f32[17,8,128]{2,1,0:T(8,128)S(1)...) custom-call(f32[39,64,128]{2,1,0:T(8,128)S(1)} %lift_own.1.refs_0_, ...), custom_call_target="tpu_custom_call", output_to_operand_aliasing={{0}: (0, {})} | custom-call | bytes 4169728 | tf_op jit(solution)/shard_map/make_messages/pallas_call | solution.py:541
  3.4 2.9 %collective-permute-start.1 = (f32[224,128]{1,0:T(8,128)S(1)}, f32[224,128]{1,0:T(8,128)S(1)}, u32[]{:S(2)}, u32[]{:S(2)}) collective-permute-start(f32[224,128]{1,0:T(8,128)S(1)} %get-tuple-element.20), channel_id=1, source_target_pairs={{0,2},{1,31},{2,4},{3,0},{4,6},{5,3},{6,8},{7,5},{8,10},{9,7},{10,... | collective-permute-start | bytes 344072 | tf_op jit(solution)/shard_map/ppermute | solution.py:614
  6.3 4.0 %collective-permute-start.2 = (f32[16,128]{1,0:T(8,128)S(1)}, f32[16,128]{1,0:T(8,128)S(1)}, u32[]{:S(2)}, u32[]{:S(2)}) collective-permute-start(f32[16,128]{1,0:T(8,128)S(1)} %get-tuple-element.21), channel_id=1, source_target_pairs={{1,4},{0,29},{2,6},{3,31},{4,8},{5,1},{6,10},{7,3},{8,12},{9,5},{1... | collective-permute-start | bytes 24584 | tf_op jit(solution)/shard_map/ppermute | solution.py:614
  10.2 1.9 %collective-permute-done.2.far = f32[16,128]{1,0:T(8,128)S(1)} collective-permute-done((f32[16,128]{1,0:T(8,128)S(1)}, f32[16,128]{1,0:T(8,128)S(1)}, u32[]{:S(2)}, u32[]{:S(2)}) %collective-permute-start.2) | collective-permute-done | bytes 8224 | tf_op jit(solution)/shard_map/ppermute | solution.py:614
  12.1 0.0 collective-permute-done.1.near
  12.1 0.6 %collective-permute-start.3 = (f32[120,128]{1,0:T(8,128)S(1)}, f32[120,128]{1,0:T(8,128)S(1)}, u32[]{:S(2)}, u32[]{:S(2)}) collective-permute-start(f32[120,128]{1,0:T(8,128)S(1)} %pack_other.1), channel_id=1, source_target_pairs={{0,1},{1,0},{2,3},{3,2},{4,5},{5,4},{6,7},{7,6},{8,9},{9,8},{10,11... | collective-permute-start | bytes 184328 | tf_op jit(solution)/shard_map/ppermute | solution.py:619
  12.7 0.4 %finish_own.1._ = f32[32,32,128]{2,1,0:T(8,128)S(1)} custom-call(f32[39,64,128]{2,1,0:T(8,128)S(1)} %get-tuple-element.16.refs_0_, f32[27,32,128]{2,1,0:T(8,128)S(1)} %get-tuple-element.17.refs_1_, f32[21,16,128]{2,1,0:T(8,128)S(1)} %get-tuple-element.18.refs_2_, f32[17,8,128]{2,1,0:T(8,128)S(1)} %get-tuple-element.19.refs_3_), custom_call_target="tpu_custom_call" | custom-call | bytes 1048576 | tf_op jit(solution)/shard_map/finish_own/pallas_call | solution.py:541
  13.1 0.2 %add_kept.1.own = f32[32,32,128]{2,1,0:T(8,128)S(1)} custom-call(f32[32,32,128]{2,1,0:T(8,128)S(1)} %finish_own.1._, f32[224,128]{1,0:T(8,128)S(1)} %collective-permute-done.1.near, f32[16,128]{1,0:T(8,128)S(1)} %collective-permute-done.2.far), custom_call_target="tpu_custom_call", output_to_operand_aliasing={{}: (0, {})} | custom-call | bytes 1048576 | tf_op jit(solution)/shard_map/add_kept/pallas_call | solution.py:541
  13.3 0.3 %collective-permute-done.3.packed = f32[120,128]{1,0:T(8,128)S(1)} collective-permute-done((f32[120,128]{1,0:T(8,128)S(1)}, f32[120,128]{1,0:T(8,128)S(1)}, u32[]{:S(2)}, u32[]{:S(2)}) %collective-permute-start.3) | collective-permute-done | bytes 61472 | tf_op jit(solution)/shard_map/ppermute | solution.py:619
  13.6 0.9 %add_swapped.1 = (f32[32,32,128]{2,1,0:T(8,128)}, f32[32,32,128]{2,1,0:T(8,128)S(1)}) custom-call(f32[32,32,128]{2,1,0:T(8,128)S(1)} %add_kept.1.own, f32[120,128]{1,0:T(8,128)S(1)} %collective-permute-done.3.packed), custom_call_target="tpu_custom_call", output_to_operand_aliasing={{1}: (0, {})} | custom-call | bytes 2097152 | tf_op jit(solution)/shard_map/add_swapped/pallas_call | solution.py:541
  (1 shorter events, 0.0 us)
Async XLA Ops:
  0.0 1.7 %copy-start = (f32[32,32,128]{2,1,0:T(8,128)S(1)}, f32[32,32,128]{2,1,0:T(8,128)}, u32[]{:S(2)}) copy-start(f32[32,32,128]{2,1,0:T(8,128)} %velocity.1) | copy-start | bytes 1572868
  0.0 2.2 %collective-permute-start = (f32[32,32,128]{2,1,0:T(8,128)}, f32[32,32,128]{2,1,0:T(8,128)S(1)}, u32[]{:S(2)}, u32[]{:S(2)}) collective-permute-start(f32[32,32,128]{2,1,0:T(8,128)} %velocity.1), channel_id=1, source_target_pairs={{0,1},{1,0},{2,3},{3,2},{4,5},{5,4},{6,7},{7,6},{8,9},{9,8},{10,11... | collective-permute-start | bytes 1572872 | tf_op jit(solution)/shard_map/ppermute | solution.py:563
  3.4 8.8 %collective-permute-start.1 = (f32[224,128]{1,0:T(8,128)S(1)}, f32[224,128]{1,0:T(8,128)S(1)}, u32[]{:S(2)}, u32[]{:S(2)}) collective-permute-start(f32[224,128]{1,0:T(8,128)S(1)} %get-tuple-element.20), channel_id=1, source_target_pairs={{0,2},{1,31},{2,4},{3,0},{4,6},{5,3},{6,8},{7,5},{8,10},{9,7},{10,... | collective-permute-start | bytes 344072 | tf_op jit(solution)/shard_map/ppermute | solution.py:614
  6.3 5.9 %collective-permute-start.2 = (f32[16,128]{1,0:T(8,128)S(1)}, f32[16,128]{1,0:T(8,128)S(1)}, u32[]{:S(2)}, u32[]{:S(2)}) collective-permute-start(f32[16,128]{1,0:T(8,128)S(1)} %get-tuple-element.21), channel_id=1, source_target_pairs={{1,4},{0,29},{2,6},{3,31},{4,8},{5,1},{6,10},{7,3},{8,12},{9,5},{1... | collective-permute-start | bytes 24584 | tf_op jit(solution)/shard_map/ppermute | solution.py:614
  12.1 1.5 %collective-permute-start.3 = (f32[120,128]{1,0:T(8,128)S(1)}, f32[120,128]{1,0:T(8,128)S(1)}, u32[]{:S(2)}, u32[]{:S(2)}) collective-permute-start(f32[120,128]{1,0:T(8,128)S(1)} %pack_other.1), channel_id=1, source_target_pairs={{0,1},{1,0},{2,3},{3,2},{4,5},{5,4},{6,7},{7,6},{8,9},{9,8},{10,11... | collective-permute-start | bytes 184328 | tf_op jit(solution)/shard_map/ppermute | solution.py:619

commit v5 on v4

--- a/solution.py
+++ b/solution.py
@@ -143,6 +143,13 @@
     return even, odd
 
 
+def even_and_odd(parts, plane):
+    return [
+        jnp.concatenate([part[plane, pl.ds(start, part.shape[1] // 2, 2), :] for part in parts])
+        for start in (0, 1)
+    ]
+
+
 def y_lift_whole(value):
     count = value.shape[0]
     row = lax.broadcasted_iota(jnp.int32, (count, 1), 0)
@@ -239,10 +246,11 @@
 
     shared = count == 2 and SHARED
     halves = 2 if shared else 1
-    (_,) = take(1)
+    first = take(1)
     others = take(count - 1)
     weights = take(2)
-    lifted = take(LEVELS)
+    first += take(count - 1)
+    lifted = [None] + take(LEVELS - 1)
     passed = take(2 if shared else len(places))
     (spread,) = take(1)
     coarse = take(LEVELS - 1)
@@ -294,7 +302,7 @@
                 step = min(block, max(1, PIECE // rows))
                 for x in range(0, block, step):
                     spread_z(source, weights[0], spread, rows, x, step)
-                spread_x(block, rows, spread, into, low, (part + 1) * rows)
+                spread_x(block, rows, spread, first[part + 1], low, 0)
         else:
             start, stop = spans[level - 1][0] // 2, spans[level - 1][1] // 2 + 1
             source = coarse[level - 1]
@@ -321,9 +329,7 @@
             at = plane - low
             split = half % 8 == 0
             if split:
-                even, odd = y_lift_split(
-                    into[at, pl.ds(0, half, 2), :], into[at, pl.ds(1, half, 2), :]
-                )
+                even, odd = y_lift_split(*even_and_odd([into] if level else first, at))
                 even = scaled(even, odd_plane, False)
             else:
                 into[at] = y_lift_whole(into[at])
@@ -358,20 +364,19 @@
 
 
 def rest_kernel(block, rows, width, *refs):
-    lifted, out, spare = refs[:LEVELS], refs[LEVELS], refs[LEVELS + 1]
+    first, lifted, (out, spare) = refs[: 1 - LEVELS - 2], refs[1 - LEVELS - 2 : -2], refs[-2:]
     for level, (low, _) in enumerate(windows(block)):
-        into, spacing, shift = lifted[level], 1 << level, shift_of(level)
-        half, mine = into.shape[1] // 2, (rows >> level) // 2
+        parts = [lifted[level - 1]] if level else first
+        spacing, shift = 1 << level, shift_of(level)
+        half, mine = sum(part.shape[1] for part in parts) // 2, (rows >> level) // 2
         for plane in range(block >> level):
             odd_plane = plane % 2 == 1
             at = plane - low
             if half % 8 == 0:
-                even, odd = y_lift_split(
-                    into[at, pl.ds(0, half, 2), :], into[at, pl.ds(1, half, 2), :]
-                )
+                even, odd = y_lift_split(*even_and_odd(parts, at))
                 even, odd = even[:mine], odd[:mine]
             else:
-                spare[plane] = y_lift_whole(into[at])
+                spare[plane] = y_lift_whole(parts[0][at])
                 even, odd = spare[plane, pl.ds(0, mine, 2), :], spare[plane, pl.ds(1, mine, 2), :]
             even, odd = scaled(even, odd_plane, False), scaled(odd, odd_plane, True)
             further = level < LEVELS - 1 and not odd_plane
@@ -455,12 +460,13 @@
     return copy
 
 
-def add_kernel(block, rows, places, last, _, *refs):
+def add_kernel(block, rows, places, last, own, *refs):
     received, refs = refs[: len(places)], refs[len(places) :]
     if last:
         whole, out, done, *clean = refs
     else:
         out, *clean = refs
+    out[...] = own[...]
     for to, arrived in zip(places, received):
         add_message(block, rows, to, arrived, 0, out, clean)
     if last:
@@ -497,7 +503,8 @@
             add_message(block, rows, side, arrived, base, out, clean)
 
 
-def keep_kernel(block, rows, _, near, far, out, *clean):
+def keep_kernel(block, rows, own, near, far, out, *clean):
+    out[...] = own[...]
     core = lax.axis_index("gy")
     add_either(block, rows, takes_right(1), 1, half_of(near, core), 0, out, clean)
     add_far(block, rows, takes_right(2), half_of(far, core), 0, out, clean)
@@ -516,6 +523,7 @@
 
 
 def swap_kernel(block, rows, one, own, packed, whole, out, done, *clean):
+    out[...] = own[...]
     add_far(block, rows, jnp.logical_not(takes_right(2)), packed, one, out, clean)
     right = jnp.logical_not(takes_right(1))
     for to, here in ((1, right), (-1, jnp.logical_not(right))):
@@ -533,7 +541,7 @@
                 copy.wait()
 
 
-def call(body, name, outs, ins, scratch=(), aliases=None, flops=0, hbm_out=()):
+def call(body, name, outs, ins, scratch=(), flops=0, hbm_out=()):
     vmem, hbm = pl.BlockSpec(memory_space=pltpu.VMEM), pl.BlockSpec(memory_space=pltpu.HBM)
     f32 = jnp.float32
     shapes = [out if isinstance(out, jax.ShapeDtypeStruct) else jax.ShapeDtypeStruct(out, f32) for out in outs]
@@ -544,7 +552,6 @@
         in_specs=[vmem] * len(ins),
         out_specs=[hbm if n in hbm_out else vmem for n in range(len(outs))],
         scratch_shapes=[pltpu.VMEM(shape, f32) if isinstance(shape, tuple) else shape for shape in scratch],
-        input_output_aliases=aliases or {},
         compiler_params=pltpu.CompilerParams(vmem_limit_bytes=VMEM_BYTES),
         cost_estimate=pl.CostEstimate(flops=flops, bytes_accessed=2 * moved, transcendentals=0),
         name=name,
@@ -571,6 +578,7 @@
         for level, (low, high) in enumerate(spans[:-1])
     ]
     spread = (block * rows, width)
+    part = (lifted[0][0], rows, width)
     owned = [(block >> level, rows >> level, width) for level in range(LEVELS)]
     lengths = {to: message(block, rows, to)[2] for to in places}
     one, two = max(lengths[1], lengths[-1]), max(lengths[2], lengths[-2])
@@ -581,7 +589,7 @@
     (first,) = call(
         functools.partial(own_kernel, block, rows),
         "lift_own",
-        [lifted[0]],
+        [part],
         [velocity, weights[0]],
         [spread],
     )
@@ -592,12 +600,11 @@
     values = call(
         functools.partial(message_kernel, block, rows, width, count, places),
         "make_messages",
-        lifted + outs,
+        [part] * (count - 1) + lifted[1:] + outs,
         [first] + others + list(weights),
         [spread] + coarse + scratch,
-        {0: 0},
     )
-    before, messages = values[:LEVELS], values[LEVELS:]
+    before, messages = [first, *values[: count + LEVELS - 2]], values[count + LEVELS - 2 :]
 
     def rest():
         return call(
@@ -623,15 +630,13 @@
             [owned[0]],
             [result, near, far],
             clean,
-            aliases={0: 0},
         )
-        whole, _ = call(
+        (whole,) = call(
             functools.partial(swap_kernel, block, rows, one),
             "add_swapped",
-            [owned[0]] * 2,
+            [owned[0]],
             [result, packed],
-            written + clean,
-            aliases={0: 1},
+            [owned[0]] + written + clean,
             hbm_out=(0,),
         )
         return whole
@@ -649,16 +654,14 @@
         [owned[0]],
         [rest()] + [received[to] for to in right],
         clean,
-        aliases={0: 0},
         flops=FIRST_FLOPS,
     )
-    whole, _ = call(
+    (whole,) = call(
         functools.partial(add_kernel, block, rows, left, True),
         "add_left",
-        [owned[0]] * 2,
+        [owned[0]],
         [result] + [received[to] for to in left],
-        written + clean,
-        aliases={0: 1},
+        [owned[0]] + written + clean,
         hbm_out=(0,),
     )
     return whole

time: 14.6 us -> 14.7 us (level)
  no operation moved by 1% of the time
where the time goes in v5:
time: 14.7 us; the launch traced here: 14.5 us
  starting transfers between devices  7.88 us (54%)
  Pallas kernels  4.38 us (30%)
  waiting for transfers between devices  2.23 us (15%)
    ppermute x2, starting transfers between devices, local(): lax.ppermute(value, ('gx', 'gy'), shared_pairs(step, around))  6.87 us
    pallas_call x7, Pallas kernels, call(): pl.pallas_call(body, out_shape=shapes, in_specs=[vmem] * len(ins), out_sp...  4.38 us
    ppermute x2, waiting for transfers between devices, local(): lax.ppermute(value, ('gx', 'gy'), shared_pairs(step, around))  1.91 us
    ppermute x1, starting transfers between devices, local(): packed = lax.ppermute(packed, 'gy', [(0, 1), (1, 0)])  0.56 us
    ppermute x1, starting transfers between devices, local(): lax.ppermute(velocity, 'gy', [(i, (i - k) % count) for i in range(count)])  0.45 us
  transfers between devices with their start and end apart: 4, of which 3 were waited for; matrix products, arithmetic and copies ran while one was open for 0% of the time, Pallas kernels for 16%

profile of v5, /device:TPU:0, one launch (start us, length us, event | category | flops | bytes accessed | tf_op | source)
XLA Modules:
  0.0 14.5 jit_solution(15659063447826038323)
XLA Ops:
  0.0 0.0 copy-start
  0.0 0.5 %collective-permute-start = (f32[32,32,128]{2,1,0:T(8,128)}, f32[32,32,128]{2,1,0:T(8,128)S(1)}, u32[]{:S(2)}, u32[]{:S(2)}) collective-permute-start(f32[32,32,128]{2,1,0:T(8,128)} %velocity.1), channel_id=1, source_target_pairs={{0,1},{1,0},{2,3},{3,2},{4,5},{5,4},{6,7},{7,6},{8,9},{9,8},{10,11... | collective-permute-start | bytes 1572872 | tf_op jit(solution)/shard_map/ppermute | solution.py:570
  0.5 1.2 %make_matrices.1 = (bf16[256,384]{1,0:T(8,128)(2,1)S(1)}, bf16[256,384]{1,0:T(8,128)(2,1)S(1)}) custom-call(), custom_call_target="tpu_custom_call" | custom-call | flops 10000000000 | bytes 1572864 | tf_op jit(solution)/shard_map/make_matrices/pallas_call | solution.py:549
  1.7 0.0 copy-done
  1.7 0.5 %lift_own.1.refs_0_ = f32[39,32,128]{2,1,0:T(8,128)S(1)} custom-call(f32[32,32,128]{2,1,0:T(8,128)S(1)} %copy-done, bf16[256,384]{1,0:T(8,128)(2,1)S(1)} %get-tuple-element.13.weights.refs_2_), custom_call_target="tpu_custom_call" | custom-call | bytes 1277952 | tf_op jit(solution)/shard_map/lift_own/pallas_call | solution.py:549
  2.1 0.1 collective-permute-done.refs_1_
  2.2 1.1 %make_messages.1 = (f32[39,32,128]{2,1,0:T(8,128)S(1)}, f32[27,32,128]{2,1,0:T(8,128)S(1)}, f32[21,16,128]{2,1,0:T(8,128)S(1)}, f32[17,8,128]{2,1,0:T(8,128)S(1)...) custom-call(f32[39,32,128]{2,1,0:T(8,128)S(1)} %lift_own.1.refs_0_, f32[32,32,128]{2,1,0:T(8,128)S(1)} %collective-permute-done.refs_1_, ...), custom_call_target="tpu_custom_call" | custom-call | bytes 2891776 | tf_op jit(solution)/shard_map/make_messages/pallas_call | solution.py:549
  3.4 2.9 %collective-permute-start.1 = (f32[224,128]{1,0:T(8,128)S(1)}, f32[224,128]{1,0:T(8,128)S(1)}, u32[]{:S(2)}, u32[]{:S(2)}) collective-permute-start(f32[224,128]{1,0:T(8,128)S(1)} %get-tuple-element.19), channel_id=1, source_target_pairs={{0,2},{1,31},{2,4},{3,0},{4,6},{5,3},{6,8},{7,5},{8,10},{9,7},{10,... | collective-permute-start | bytes 344072 | tf_op jit(solution)/shard_map/ppermute | solution.py:621
  6.3 4.0 %collective-permute-start.2 = (f32[16,128]{1,0:T(8,128)S(1)}, f32[16,128]{1,0:T(8,128)S(1)}, u32[]{:S(2)}, u32[]{:S(2)}) collective-permute-start(f32[16,128]{1,0:T(8,128)S(1)} %get-tuple-element.20), channel_id=1, source_target_pairs={{1,4},{0,29},{2,6},{3,31},{4,8},{5,1},{6,10},{7,3},{8,12},{9,5},{1... | collective-permute-start | bytes 24584 | tf_op jit(solution)/shard_map/ppermute | solution.py:621
  10.2 1.9 %collective-permute-done.2.far = f32[16,128]{1,0:T(8,128)S(1)} collective-permute-done((f32[16,128]{1,0:T(8,128)S(1)}, f32[16,128]{1,0:T(8,128)S(1)}, u32[]{:S(2)}, u32[]{:S(2)}) %collective-permute-start.2) | collective-permute-done | bytes 8224 | tf_op jit(solution)/shard_map/ppermute | solution.py:621
  12.1 0.0 collective-permute-done.1.near
  12.1 0.6 %collective-permute-start.3 = (f32[120,128]{1,0:T(8,128)S(1)}, f32[120,128]{1,0:T(8,128)S(1)}, u32[]{:S(2)}, u32[]{:S(2)}) collective-permute-start(f32[120,128]{1,0:T(8,128)S(1)} %pack_other.1), channel_id=1, source_target_pairs={{0,1},{1,0},{2,3},{3,2},{4,5},{5,4},{6,7},{7,6},{8,9},{9,8},{10,11... | collective-permute-start | bytes 184328 | tf_op jit(solution)/shard_map/ppermute | solution.py:626
  12.7 0.4 %finish_own.1.own = f32[32,32,128]{2,1,0:T(8,128)S(1)} custom-call(f32[39,32,128]{2,1,0:T(8,128)S(1)} %lift_own.1.refs_0_, f32[39,32,128]{2,1,0:T(8,128)S(1)} %get-tuple-element.15.refs_1_, f32[27,32,128]{2,1,0:T(8,128)S(1)} %get-tuple-element.16.refs_2_, f32[21,16,128]{2,1,0:T(8,128)S(1)} %get-tuple-element.17.refs_3_, ...), custom_call_target="tpu_custom_call" | custom-call | bytes 1048576 | tf_op jit(solution)/shard_map/finish_own/pallas_call | solution.py:549
  13.1 0.2 %add_kept.1.own = f32[32,32,128]{2,1,0:T(8,128)S(1)} custom-call(f32[32,32,128]{2,1,0:T(8,128)S(1)} %finish_own.1.own, f32[224,128]{1,0:T(8,128)S(1)} %collective-permute-done.1.near, f32[16,128]{1,0:T(8,128)S(1)} %collective-permute-done.2.far), custom_call_target="tpu_custom_call" | custom-call | bytes 1048576 | tf_op jit(solution)/shard_map/add_kept/pallas_call | solution.py:549
  13.3 0.3 %collective-permute-done.3.packed = f32[120,128]{1,0:T(8,128)S(1)} collective-permute-done((f32[120,128]{1,0:T(8,128)S(1)}, f32[120,128]{1,0:T(8,128)S(1)}, u32[]{:S(2)}, u32[]{:S(2)}) %collective-permute-start.3) | collective-permute-done | bytes 61472 | tf_op jit(solution)/shard_map/ppermute | solution.py:626
  13.6 0.9 %add_swapped.1 = f32[32,32,128]{2,1,0:T(8,128)} custom-call(f32[32,32,128]{2,1,0:T(8,128)S(1)} %add_kept.1.own, f32[120,128]{1,0:T(8,128)S(1)} %collective-permute-done.3.packed), custom_call_target="tpu_custom_call" | custom-call | bytes 1048576 | tf_op jit(solution)/shard_map/add_swapped/pallas_call | solution.py:549
  (1 shorter events, 0.0 us)
Async XLA Ops:
  0.0 1.7 %copy-start = (f32[32,32,128]{2,1,0:T(8,128)S(1)}, f32[32,32,128]{2,1,0:T(8,128)}, u32[]{:S(2)}) copy-start(f32[32,32,128]{2,1,0:T(8,128)} %velocity.1) | copy-start | bytes 1572868
  0.0 2.2 %collective-permute-start = (f32[32,32,128]{2,1,0:T(8,128)}, f32[32,32,128]{2,1,0:T(8,128)S(1)}, u32[]{:S(2)}, u32[]{:S(2)}) collective-permute-start(f32[32,32,128]{2,1,0:T(8,128)} %velocity.1), channel_id=1, source_target_pairs={{0,1},{1,0},{2,3},{3,2},{4,5},{5,4},{6,7},{7,6},{8,9},{9,8},{10,11... | collective-permute-start | bytes 1572872 | tf_op jit(solution)/shard_map/ppermute | solution.py:570
  3.4 8.8 %collective-permute-start.1 = (f32[224,128]{1,0:T(8,128)S(1)}, f32[224,128]{1,0:T(8,128)S(1)}, u32[]{:S(2)}, u32[]{:S(2)}) collective-permute-start(f32[224,128]{1,0:T(8,128)S(1)} %get-tuple-element.19), channel_id=1, source_target_pairs={{0,2},{1,31},{2,4},{3,0},{4,6},{5,3},{6,8},{7,5},{8,10},{9,7},{10,... | collective-permute-start | bytes 344072 | tf_op jit(solution)/shard_map/ppermute | solution.py:621
  6.3 5.9 %collective-permute-start.2 = (f32[16,128]{1,0:T(8,128)S(1)}, f32[16,128]{1,0:T(8,128)S(1)}, u32[]{:S(2)}, u32[]{:S(2)}) collective-permute-start(f32[16,128]{1,0:T(8,128)S(1)} %get-tuple-element.20), channel_id=1, source_target_pairs={{1,4},{0,29},{2,6},{3,31},{4,8},{5,1},{6,10},{7,3},{8,12},{9,5},{1... | collective-permute-start | bytes 24584 | tf_op jit(solution)/shard_map/ppermute | solution.py:621
  12.1 1.5 %collective-permute-start.3 = (f32[120,128]{1,0:T(8,128)S(1)}, f32[120,128]{1,0:T(8,128)S(1)}, u32[]{:S(2)}, u32[]{:S(2)}) collective-permute-start(f32[120,128]{1,0:T(8,128)S(1)} %pack_other.1), channel_id=1, source_target_pairs={{0,1},{1,0},{2,3},{3,2},{4,5},{5,4},{6,7},{7,6},{8,9},{9,8},{10,11... | collective-permute-start | bytes 184328 | tf_op jit(solution)/shard_map/ppermute | solution.py:626

commit v6 on v5

--- a/solution.py
+++ b/solution.py
@@ -209,7 +209,7 @@
 
 
 def right_source(step, place, last):
-    return place == last if step == 1 else (place == 0) | (place == last - 1)
+    return place == (last if step == 1 else last - 1)
 
 
 def right_target(step, place):

time: 14.7 us -> 14.7 us (level)
  waiting for transfers between devices: 2.23 us -> 4.67 us
  starting transfers between devices: 7.88 us -> 5.45 us
    ppermute x2, starting transfers between devices: 6.87 us -> 4.44 us  [local(): lax.ppermute(value, ('gx', 'gy'), shared_pairs(step, around))]
    ppermute x2, waiting for transfers between devices: 1.91 us -> 4.34 us  [local(): lax.ppermute(value, ('gx', 'gy'), shared_pairs(step, around))]
where the time goes in v6:
time: 14.7 us; the launch traced here: 14.5 us
  starting transfers between devices  5.45 us (37%)
  waiting for transfers between devices  4.67 us (32%)
  Pallas kernels  4.38 us (30%)
    ppermute x2, starting transfers between devices, local(): lax.ppermute(value, ('gx', 'gy'), shared_pairs(step, around))  4.44 us
    pallas_call x7, Pallas kernels, call(): pl.pallas_call(body, out_shape=shapes, in_specs=[vmem] * len(ins), out_sp...  4.38 us
    ppermute x2, waiting for transfers between devices, local(): lax.ppermute(value, ('gx', 'gy'), shared_pairs(step, around))  4.34 us
    ppermute x1, starting transfers between devices, local(): packed = lax.ppermute(packed, 'gy', [(0, 1), (1, 0)])  0.56 us
    ppermute x1, starting transfers between devices, local(): lax.ppermute(velocity, 'gy', [(i, (i - k) % count) for i in range(count)])  0.45 us
  transfers between devices with their start and end apart: 4, of which 3 were waited for; matrix products, arithmetic and copies ran while one was open for 0% of the time, Pallas kernels for 16%

profile of v6, /device:TPU:0, one launch (start us, length us, event | category | flops | bytes accessed | tf_op | source)
XLA Modules:
  0.0 14.5 jit_solution(8277605274223325337)
XLA Ops:
  0.0 0.0 copy-start
  0.0 0.5 %collective-permute-start = (f32[32,32,128]{2,1,0:T(8,128)}, f32[32,32,128]{2,1,0:T(8,128)S(1)}, u32[]{:S(2)}, u32[]{:S(2)}) collective-permute-start(f32[32,32,128]{2,1,0:T(8,128)} %velocity.1), channel_id=1, source_target_pairs={{0,1},{1,0},{2,3},{3,2},{4,5},{5,4},{6,7},{7,6},{8,9},{9,8},{10,11... | collective-permute-start | bytes 1572872 | tf_op jit(solution)/shard_map/ppermute | solution.py:570
  0.5 1.2 %make_matrices.1 = (bf16[256,384]{1,0:T(8,128)(2,1)S(1)}, bf16[256,384]{1,0:T(8,128)(2,1)S(1)}) custom-call(), custom_call_target="tpu_custom_call" | custom-call | flops 10000000000 | bytes 1572864 | tf_op jit(solution)/shard_map/make_matrices/pallas_call | solution.py:549
  1.7 0.0 copy-done
  1.7 0.5 %lift_own.1.refs_0_ = f32[39,32,128]{2,1,0:T(8,128)S(1)} custom-call(f32[32,32,128]{2,1,0:T(8,128)S(1)} %copy-done, bf16[256,384]{1,0:T(8,128)(2,1)S(1)} %get-tuple-element.13.weights.refs_2_), custom_call_target="tpu_custom_call" | custom-call | bytes 1277952 | tf_op jit(solution)/shard_map/lift_own/pallas_call | solution.py:549
  2.1 0.1 collective-permute-done.refs_1_
  2.2 1.1 %make_messages.1 = (f32[39,32,128]{2,1,0:T(8,128)S(1)}, f32[27,32,128]{2,1,0:T(8,128)S(1)}, f32[21,16,128]{2,1,0:T(8,128)S(1)}, f32[17,8,128]{2,1,0:T(8,128)S(1)...) custom-call(f32[39,32,128]{2,1,0:T(8,128)S(1)} %lift_own.1.refs_0_, f32[32,32,128]{2,1,0:T(8,128)S(1)} %collective-permute-done.refs_1_, ...), custom_call_target="tpu_custom_call" | custom-call | bytes 2891776 | tf_op jit(solution)/shard_map/make_messages/pallas_call | solution.py:549
  3.4 2.9 %collective-permute-start.1 = (f32[224,128]{1,0:T(8,128)S(1)}, f32[224,128]{1,0:T(8,128)S(1)}, u32[]{:S(2)}, u32[]{:S(2)}) collective-permute-start(f32[224,128]{1,0:T(8,128)S(1)} %get-tuple-element.19), channel_id=1, source_target_pairs={{0,2},{1,31},{2,4},{3,0},{4,6},{5,3},{6,8},{7,5},{8,10},{9,7},{10,... | collective-permute-start | bytes 344072 | tf_op jit(solution)/shard_map/ppermute | solution.py:621
  6.3 1.5 %collective-permute-start.2 = (f32[16,128]{1,0:T(8,128)S(1)}, f32[16,128]{1,0:T(8,128)S(1)}, u32[]{:S(2)}, u32[]{:S(2)}) collective-permute-start(f32[16,128]{1,0:T(8,128)S(1)} %get-tuple-element.20), channel_id=1, source_target_pairs={{0,4},{1,29},{2,6},{3,31},{4,8},{5,1},{6,10},{7,3},{8,12},{9,5},{1... | collective-permute-start | bytes 24584 | tf_op jit(solution)/shard_map/ppermute | solution.py:621
  7.8 4.3 %collective-permute-done.2.far = f32[16,128]{1,0:T(8,128)S(1)} collective-permute-done((f32[16,128]{1,0:T(8,128)S(1)}, f32[16,128]{1,0:T(8,128)S(1)}, u32[]{:S(2)}, u32[]{:S(2)}) %collective-permute-start.2) | collective-permute-done | bytes 8224 | tf_op jit(solution)/shard_map/ppermute | solution.py:621
  12.1 0.0 collective-permute-done.1.near
  12.1 0.6 %collective-permute-start.3 = (f32[120,128]{1,0:T(8,128)S(1)}, f32[120,128]{1,0:T(8,128)S(1)}, u32[]{:S(2)}, u32[]{:S(2)}) collective-permute-start(f32[120,128]{1,0:T(8,128)S(1)} %pack_other.1), channel_id=1, source_target_pairs={{0,1},{1,0},{2,3},{3,2},{4,5},{5,4},{6,7},{7,6},{8,9},{9,8},{10,11... | collective-permute-start | bytes 184328 | tf_op jit(solution)/shard_map/ppermute | solution.py:626
  12.7 0.4 %finish_own.1.own = f32[32,32,128]{2,1,0:T(8,128)S(1)} custom-call(f32[39,32,128]{2,1,0:T(8,128)S(1)} %lift_own.1.refs_0_, f32[39,32,128]{2,1,0:T(8,128)S(1)} %get-tuple-element.15.refs_1_, f32[27,32,128]{2,1,0:T(8,128)S(1)} %get-tuple-element.16.refs_2_, f32[21,16,128]{2,1,0:T(8,128)S(1)} %get-tuple-element.17.refs_3_, ...), custom_call_target="tpu_custom_call" | custom-call | bytes 1048576 | tf_op jit(solution)/shard_map/finish_own/pallas_call | solution.py:549
  13.1 0.2 %add_kept.1.own = f32[32,32,128]{2,1,0:T(8,128)S(1)} custom-call(f32[32,32,128]{2,1,0:T(8,128)S(1)} %finish_own.1.own, f32[224,128]{1,0:T(8,128)S(1)} %collective-permute-done.1.near, f32[16,128]{1,0:T(8,128)S(1)} %collective-permute-done.2.far), custom_call_target="tpu_custom_call" | custom-call | bytes 1048576 | tf_op jit(solution)/shard_map/add_kept/pallas_call | solution.py:549
  13.3 0.3 %collective-permute-done.3.packed = f32[120,128]{1,0:T(8,128)S(1)} collective-permute-done((f32[120,128]{1,0:T(8,128)S(1)}, f32[120,128]{1,0:T(8,128)S(1)}, u32[]{:S(2)}, u32[]{:S(2)}) %collective-permute-start.3) | collective-permute-done | bytes 61472 | tf_op jit(solution)/shard_map/ppermute | solution.py:626
  13.6 0.9 %add_swapped.1 = f32[32,32,128]{2,1,0:T(8,128)} custom-call(f32[32,32,128]{2,1,0:T(8,128)S(1)} %add_kept.1.own, f32[120,128]{1,0:T(8,128)S(1)} %collective-permute-done.3.packed), custom_call_target="tpu_custom_call" | custom-call | bytes 1048576 | tf_op jit(solution)/shard_map/add_swapped/pallas_call | solution.py:549
  (1 shorter events, 0.0 us)
Async XLA Ops:
  0.0 1.7 %copy-start = (f32[32,32,128]{2,1,0:T(8,128)S(1)}, f32[32,32,128]{2,1,0:T(8,128)}, u32[]{:S(2)}) copy-start(f32[32,32,128]{2,1,0:T(8,128)} %velocity.1) | copy-start | bytes 1572868
  0.0 2.2 %collective-permute-start = (f32[32,32,128]{2,1,0:T(8,128)}, f32[32,32,128]{2,1,0:T(8,128)S(1)}, u32[]{:S(2)}, u32[]{:S(2)}) collective-permute-start(f32[32,32,128]{2,1,0:T(8,128)} %velocity.1), channel_id=1, source_target_pairs={{0,1},{1,0},{2,3},{3,2},{4,5},{5,4},{6,7},{7,6},{8,9},{9,8},{10,11... | collective-permute-start | bytes 1572872 | tf_op jit(solution)/shard_map/ppermute | solution.py:570
  3.4 8.8 %collective-permute-start.1 = (f32[224,128]{1,0:T(8,128)S(1)}, f32[224,128]{1,0:T(8,128)S(1)}, u32[]{:S(2)}, u32[]{:S(2)}) collective-permute-start(f32[224,128]{1,0:T(8,128)S(1)} %get-tuple-element.19), channel_id=1, source_target_pairs={{0,2},{1,31},{2,4},{3,0},{4,6},{5,3},{6,8},{7,5},{8,10},{9,7},{10,... | collective-permute-start | bytes 344072 | tf_op jit(solution)/shard_map/ppermute | solution.py:621
  6.3 5.9 %collective-permute-start.2 = (f32[16,128]{1,0:T(8,128)S(1)}, f32[16,128]{1,0:T(8,128)S(1)}, u32[]{:S(2)}, u32[]{:S(2)}) collective-permute-start(f32[16,128]{1,0:T(8,128)S(1)} %get-tuple-element.20), channel_id=1, source_target_pairs={{0,4},{1,29},{2,6},{3,31},{4,8},{5,1},{6,10},{7,3},{8,12},{9,5},{1... | collective-permute-start | bytes 24584 | tf_op jit(solution)/shard_map/ppermute | solution.py:621
  12.1 1.5 %collective-permute-start.3 = (f32[120,128]{1,0:T(8,128)S(1)}, f32[120,128]{1,0:T(8,128)S(1)}, u32[]{:S(2)}, u32[]{:S(2)}) collective-permute-start(f32[120,128]{1,0:T(8,128)S(1)} %pack_other.1), channel_id=1, source_target_pairs={{0,1},{1,0},{2,3},{3,2},{4,5},{5,4},{6,7},{7,6},{8,9},{9,8},{10,11... | collective-permute-start | bytes 184328 | tf_op jit(solution)/shard_map/ppermute | solution.py:626

commit v7 on v5

--- a/solution.py
+++ b/solution.py
@@ -456,7 +456,7 @@
     size = out.shape[0] // parts
     here = pl.ds(part * size, size)
     copy = pltpu.make_async_copy(out.at[here], whole.at[here], done.at[part])
-    copy.start()
+    copy.start(priority=part)
     return copy
 
 

time: 14.7 us -> 14.7 us (level)
  no operation moved by 1% of the time
where the time goes in v7:
time: 14.7 us; the launch traced here: 14.6 us
  starting transfers between devices  7.88 us (54%)
  Pallas kernels  4.4 us (30%)
  waiting for transfers between devices  2.23 us (15%)
    ppermute x2, starting transfers between devices, local(): lax.ppermute(value, ('gx', 'gy'), shared_pairs(step, around))  6.87 us
    pallas_call x7, Pallas kernels, call(): pl.pallas_call(body, out_shape=shapes, in_specs=[vmem] * len(ins), out_sp...  4.4 us
    ppermute x2, waiting for transfers between devices, local(): lax.ppermute(value, ('gx', 'gy'), shared_pairs(step, around))  1.91 us
    ppermute x1, starting transfers between devices, local(): packed = lax.ppermute(packed, 'gy', [(0, 1), (1, 0)])  0.56 us
    ppermute x1, starting transfers between devices, local(): lax.ppermute(velocity, 'gy', [(i, (i - k) % count) for i in range(count)])  0.45 us
  transfers between devices with their start and end apart: 4, of which 3 were waited for; matrix products, arithmetic and copies ran while one was open for 0% of the time, Pallas kernels for 16%

profile of v7, /device:TPU:0, one launch (start us, length us, event | category | flops | bytes accessed | tf_op | source)
XLA Modules:
  0.0 14.6 jit_solution(16627652034102650081)
XLA Ops:
  0.0 0.0 copy-start
  0.0 0.5 %collective-permute-start = (f32[32,32,128]{2,1,0:T(8,128)}, f32[32,32,128]{2,1,0:T(8,128)S(1)}, u32[]{:S(2)}, u32[]{:S(2)}) collective-permute-start(f32[32,32,128]{2,1,0:T(8,128)} %velocity.1), channel_id=1, source_target_pairs={{0,1},{1,0},{2,3},{3,2},{4,5},{5,4},{6,7},{7,6},{8,9},{9,8},{10,11... | collective-permute-start | bytes 1572872 | tf_op jit(solution)/shard_map/ppermute | solution.py:570
  0.5 1.2 %make_matrices.1 = (bf16[256,384]{1,0:T(8,128)(2,1)S(1)}, bf16[256,384]{1,0:T(8,128)(2,1)S(1)}) custom-call(), custom_call_target="tpu_custom_call" | custom-call | flops 10000000000 | bytes 1572864 | tf_op jit(solution)/shard_map/make_matrices/pallas_call | solution.py:549
  1.7 0.0 copy-done
  1.7 0.5 %lift_own.1.refs_0_ = f32[39,32,128]{2,1,0:T(8,128)S(1)} custom-call(f32[32,32,128]{2,1,0:T(8,128)S(1)} %copy-done, bf16[256,384]{1,0:T(8,128)(2,1)S(1)} %get-tuple-element.13.weights.refs_2_), custom_call_target="tpu_custom_call" | custom-call | bytes 1277952 | tf_op jit(solution)/shard_map/lift_own/pallas_call | solution.py:549
  2.1 0.1 collective-permute-done.refs_1_
  2.2 1.1 %make_messages.1 = (f32[39,32,128]{2,1,0:T(8,128)S(1)}, f32[27,32,128]{2,1,0:T(8,128)S(1)}, f32[21,16,128]{2,1,0:T(8,128)S(1)}, f32[17,8,128]{2,1,0:T(8,128)S(1)...) custom-call(f32[39,32,128]{2,1,0:T(8,128)S(1)} %lift_own.1.refs_0_, f32[32,32,128]{2,1,0:T(8,128)S(1)} %collective-permute-done.refs_1_, ...), custom_call_target="tpu_custom_call" | custom-call | bytes 2891776 | tf_op jit(solution)/shard_map/make_messages/pallas_call | solution.py:549
  3.4 2.9 %collective-permute-start.1 = (f32[224,128]{1,0:T(8,128)S(1)}, f32[224,128]{1,0:T(8,128)S(1)}, u32[]{:S(2)}, u32[]{:S(2)}) collective-permute-start(f32[224,128]{1,0:T(8,128)S(1)} %get-tuple-element.19), channel_id=1, source_target_pairs={{0,2},{1,31},{2,4},{3,0},{4,6},{5,3},{6,8},{7,5},{8,10},{9,7},{10,... | collective-permute-start | bytes 344072 | tf_op jit(solution)/shard_map/ppermute | solution.py:621
  6.3 4.0 %collective-permute-start.2 = (f32[16,128]{1,0:T(8,128)S(1)}, f32[16,128]{1,0:T(8,128)S(1)}, u32[]{:S(2)}, u32[]{:S(2)}) collective-permute-start(f32[16,128]{1,0:T(8,128)S(1)} %get-tuple-element.20), channel_id=1, source_target_pairs={{1,4},{0,29},{2,6},{3,31},{4,8},{5,1},{6,10},{7,3},{8,12},{9,5},{1... | collective-permute-start | bytes 24584 | tf_op jit(solution)/shard_map/ppermute | solution.py:621
  10.2 1.9 %collective-permute-done.2.far = f32[16,128]{1,0:T(8,128)S(1)} collective-permute-done((f32[16,128]{1,0:T(8,128)S(1)}, f32[16,128]{1,0:T(8,128)S(1)}, u32[]{:S(2)}, u32[]{:S(2)}) %collective-permute-start.2) | collective-permute-done | bytes 8224 | tf_op jit(solution)/shard_map/ppermute | solution.py:621
  12.1 0.0 collective-permute-done.1.near
  12.1 0.6 %collective-permute-start.3 = (f32[120,128]{1,0:T(8,128)S(1)}, f32[120,128]{1,0:T(8,128)S(1)}, u32[]{:S(2)}, u32[]{:S(2)}) collective-permute-start(f32[120,128]{1,0:T(8,128)S(1)} %pack_other.1), channel_id=1, source_target_pairs={{0,1},{1,0},{2,3},{3,2},{4,5},{5,4},{6,7},{7,6},{8,9},{9,8},{10,11... | collective-permute-start | bytes 184328 | tf_op jit(solution)/shard_map/ppermute | solution.py:626
  12.7 0.4 %finish_own.1.own = f32[32,32,128]{2,1,0:T(8,128)S(1)} custom-call(f32[39,32,128]{2,1,0:T(8,128)S(1)} %lift_own.1.refs_0_, f32[39,32,128]{2,1,0:T(8,128)S(1)} %get-tuple-element.15.refs_1_, f32[27,32,128]{2,1,0:T(8,128)S(1)} %get-tuple-element.16.refs_2_, f32[21,16,128]{2,1,0:T(8,128)S(1)} %get-tuple-element.17.refs_3_, ...), custom_call_target="tpu_custom_call" | custom-call | bytes 1048576 | tf_op jit(solution)/shard_map/finish_own/pallas_call | solution.py:549
  13.1 0.2 %add_kept.1.own = f32[32,32,128]{2,1,0:T(8,128)S(1)} custom-call(f32[32,32,128]{2,1,0:T(8,128)S(1)} %finish_own.1.own, f32[224,128]{1,0:T(8,128)S(1)} %collective-permute-done.1.near, f32[16,128]{1,0:T(8,128)S(1)} %collective-permute-done.2.far), custom_call_target="tpu_custom_call" | custom-call | bytes 1048576 | tf_op jit(solution)/shard_map/add_kept/pallas_call | solution.py:549
  13.3 0.3 %collective-permute-done.3.packed = f32[120,128]{1,0:T(8,128)S(1)} collective-permute-done((f32[120,128]{1,0:T(8,128)S(1)}, f32[120,128]{1,0:T(8,128)S(1)}, u32[]{:S(2)}, u32[]{:S(2)}) %collective-permute-start.3) | collective-permute-done | bytes 61472 | tf_op jit(solution)/shard_map/ppermute | solution.py:626
  13.6 1.0 %add_swapped.1 = f32[32,32,128]{2,1,0:T(8,128)} custom-call(f32[32,32,128]{2,1,0:T(8,128)S(1)} %add_kept.1.own, f32[120,128]{1,0:T(8,128)S(1)} %collective-permute-done.3.packed), custom_call_target="tpu_custom_call" | custom-call | bytes 1048576 | tf_op jit(solution)/shard_map/add_swapped/pallas_call | solution.py:549
  (1 shorter events, 0.0 us)
Async XLA Ops:
  0.0 1.7 %copy-start = (f32[32,32,128]{2,1,0:T(8,128)S(1)}, f32[32,32,128]{2,1,0:T(8,128)}, u32[]{:S(2)}) copy-start(f32[32,32,128]{2,1,0:T(8,128)} %velocity.1) | copy-start | bytes 1572868
  0.0 2.2 %collective-permute-start = (f32[32,32,128]{2,1,0:T(8,128)}, f32[32,32,128]{2,1,0:T(8,128)S(1)}, u32[]{:S(2)}, u32[]{:S(2)}) collective-permute-start(f32[32,32,128]{2,1,0:T(8,128)} %velocity.1), channel_id=1, source_target_pairs={{0,1},{1,0},{2,3},{3,2},{4,5},{5,4},{6,7},{7,6},{8,9},{9,8},{10,11... | collective-permute-start | bytes 1572872 | tf_op jit(solution)/shard_map/ppermute | solution.py:570
  3.4 8.8 %collective-permute-start.1 = (f32[224,128]{1,0:T(8,128)S(1)}, f32[224,128]{1,0:T(8,128)S(1)}, u32[]{:S(2)}, u32[]{:S(2)}) collective-permute-start(f32[224,128]{1,0:T(8,128)S(1)} %get-tuple-element.19), channel_id=1, source_target_pairs={{0,2},{1,31},{2,4},{3,0},{4,6},{5,3},{6,8},{7,5},{8,10},{9,7},{10,... | collective-permute-start | bytes 344072 | tf_op jit(solution)/shard_map/ppermute | solution.py:621
  6.3 5.9 %collective-permute-start.2 = (f32[16,128]{1,0:T(8,128)S(1)}, f32[16,128]{1,0:T(8,128)S(1)}, u32[]{:S(2)}, u32[]{:S(2)}) collective-permute-start(f32[16,128]{1,0:T(8,128)S(1)} %get-tuple-element.20), channel_id=1, source_target_pairs={{1,4},{0,29},{2,6},{3,31},{4,8},{5,1},{6,10},{7,3},{8,12},{9,5},{1... | collective-permute-start | bytes 24584 | tf_op jit(solution)/shard_map/ppermute | solution.py:621
  12.1 1.5 %collective-permute-start.3 = (f32[120,128]{1,0:T(8,128)S(1)}, f32[120,128]{1,0:T(8,128)S(1)}, u32[]{:S(2)}, u32[]{:S(2)}) collective-permute-start(f32[120,128]{1,0:T(8,128)S(1)} %pack_other.1), channel_id=1, source_target_pairs={{0,1},{1,0},{2,3},{3,2},{4,5},{5,4},{6,7},{7,6},{8,9},{9,8},{10,11... | collective-permute-start | bytes 184328 | tf_op jit(solution)/shard_map/ppermute | solution.py:626

commit v8 on v5

--- a/solution.py
+++ b/solution.py
@@ -13,7 +13,7 @@
 SCALE = 1.149604398
 VMEM_BYTES = 24 * 2**20
 FIRST_FLOPS = 10**10
-PIECE = 1024
+PIECE = 256
 SHARED = True
 
 

time: 14.7 us -> 14.7 us (level)
  no operation moved by 1% of the time
where the time goes in v8:
time: 14.7 us; the launch traced here: 14.6 us
  starting transfers between devices  7.89 us (54%)
  Pallas kernels  4.41 us (30%)
  waiting for transfers between devices  2.23 us (15%)
    ppermute x2, starting transfers between devices, local(): lax.ppermute(value, ('gx', 'gy'), shared_pairs(step, around))  6.87 us
    pallas_call x7, Pallas kernels, call(): pl.pallas_call(body, out_shape=shapes, in_specs=[vmem] * len(ins), out_sp...  4.41 us
    ppermute x2, waiting for transfers between devices, local(): lax.ppermute(value, ('gx', 'gy'), shared_pairs(step, around))  1.9 us
    ppermute x1, starting transfers between devices, local(): packed = lax.ppermute(packed, 'gy', [(0, 1), (1, 0)])  0.56 us
    ppermute x1, starting transfers between devices, local(): lax.ppermute(velocity, 'gy', [(i, (i - k) % count) for i in range(count)])  0.45 us
  transfers between devices with their start and end apart: 4, of which 3 were waited for; matrix products, arithmetic and copies ran while one was open for 0% of the time, Pallas kernels for 16%

profile of v8, /device:TPU:0, one launch (start us, length us, event | category | flops | bytes accessed | tf_op | source)
XLA Modules:
  0.0 14.6 jit_solution(17531552557183186468)
XLA Ops:
  0.0 0.0 copy-start
  0.0 0.5 %collective-permute-start = (f32[32,32,128]{2,1,0:T(8,128)}, f32[32,32,128]{2,1,0:T(8,128)S(1)}, u32[]{:S(2)}, u32[]{:S(2)}) collective-permute-start(f32[32,32,128]{2,1,0:T(8,128)} %velocity.1), channel_id=1, source_target_pairs={{0,1},{1,0},{2,3},{3,2},{4,5},{5,4},{6,7},{7,6},{8,9},{9,8},{10,11... | collective-permute-start | bytes 1572872 | tf_op jit(solution)/shard_map/ppermute | solution.py:570
  0.5 1.2 %make_matrices.1 = (bf16[256,384]{1,0:T(8,128)(2,1)S(1)}, bf16[256,384]{1,0:T(8,128)(2,1)S(1)}) custom-call(), custom_call_target="tpu_custom_call" | custom-call | flops 10000000000 | bytes 1572864 | tf_op jit(solution)/shard_map/make_matrices/pallas_call | solution.py:549
  1.7 0.0 copy-done
  1.7 0.5 %lift_own.1.refs_0_ = f32[39,32,128]{2,1,0:T(8,128)S(1)} custom-call(f32[32,32,128]{2,1,0:T(8,128)S(1)} %copy-done, bf16[256,384]{1,0:T(8,128)(2,1)S(1)} %get-tuple-element.13.weights.refs_2_), custom_call_target="tpu_custom_call" | custom-call | bytes 1277952 | tf_op jit(solution)/shard_map/lift_own/pallas_call | solution.py:549
  2.1 0.1 collective-permute-done.refs_1_
  2.2 1.2 %make_messages.1 = (f32[39,32,128]{2,1,0:T(8,128)S(1)}, f32[27,32,128]{2,1,0:T(8,128)S(1)}, f32[21,16,128]{2,1,0:T(8,128)S(1)}, f32[17,8,128]{2,1,0:T(8,128)S(1)...) custom-call(f32[39,32,128]{2,1,0:T(8,128)S(1)} %lift_own.1.refs_0_, f32[32,32,128]{2,1,0:T(8,128)S(1)} %collective-permute-done.refs_1_, ...), custom_call_target="tpu_custom_call" | custom-call | bytes 2891776 | tf_op jit(solution)/shard_map/make_messages/pallas_call | solution.py:549
  3.4 2.9 %collective-permute-start.1 = (f32[224,128]{1,0:T(8,128)S(1)}, f32[224,128]{1,0:T(8,128)S(1)}, u32[]{:S(2)}, u32[]{:S(2)}) collective-permute-start(f32[224,128]{1,0:T(8,128)S(1)} %get-tuple-element.19), channel_id=1, source_target_pairs={{0,2},{1,31},{2,4},{3,0},{4,6},{5,3},{6,8},{7,5},{8,10},{9,7},{10,... | collective-permute-start | bytes 344072 | tf_op jit(solution)/shard_map/ppermute | solution.py:621
  6.3 4.0 %collective-permute-start.2 = (f32[16,128]{1,0:T(8,128)S(1)}, f32[16,128]{1,0:T(8,128)S(1)}, u32[]{:S(2)}, u32[]{:S(2)}) collective-permute-start(f32[16,128]{1,0:T(8,128)S(1)} %get-tuple-element.20), channel_id=1, source_target_pairs={{1,4},{0,29},{2,6},{3,31},{4,8},{5,1},{6,10},{7,3},{8,12},{9,5},{1... | collective-permute-start | bytes 24584 | tf_op jit(solution)/shard_map/ppermute | solution.py:621
  10.3 1.9 %collective-permute-done.2.far = f32[16,128]{1,0:T(8,128)S(1)} collective-permute-done((f32[16,128]{1,0:T(8,128)S(1)}, f32[16,128]{1,0:T(8,128)S(1)}, u32[]{:S(2)}, u32[]{:S(2)}) %collective-permute-start.2) | collective-permute-done | bytes 8224 | tf_op jit(solution)/shard_map/ppermute | solution.py:621
  12.2 0.0 collective-permute-done.1.near
  12.2 0.6 %collective-permute-start.3 = (f32[120,128]{1,0:T(8,128)S(1)}, f32[120,128]{1,0:T(8,128)S(1)}, u32[]{:S(2)}, u32[]{:S(2)}) collective-permute-start(f32[120,128]{1,0:T(8,128)S(1)} %pack_other.1), channel_id=1, source_target_pairs={{0,1},{1,0},{2,3},{3,2},{4,5},{5,4},{6,7},{7,6},{8,9},{9,8},{10,11... | collective-permute-start | bytes 184328 | tf_op jit(solution)/shard_map/ppermute | solution.py:626
  12.7 0.4 %finish_own.1.own = f32[32,32,128]{2,1,0:T(8,128)S(1)} custom-call(f32[39,32,128]{2,1,0:T(8,128)S(1)} %lift_own.1.refs_0_, f32[39,32,128]{2,1,0:T(8,128)S(1)} %get-tuple-element.15.refs_1_, f32[27,32,128]{2,1,0:T(8,128)S(1)} %get-tuple-element.16.refs_2_, f32[21,16,128]{2,1,0:T(8,128)S(1)} %get-tuple-element.17.refs_3_, ...), custom_call_target="tpu_custom_call" | custom-call | bytes 1048576 | tf_op jit(solution)/shard_map/finish_own/pallas_call | solution.py:549
  13.2 0.2 %add_kept.1.own = f32[32,32,128]{2,1,0:T(8,128)S(1)} custom-call(f32[32,32,128]{2,1,0:T(8,128)S(1)} %finish_own.1.own, f32[224,128]{1,0:T(8,128)S(1)} %collective-permute-done.1.near, f32[16,128]{1,0:T(8,128)S(1)} %collective-permute-done.2.far), custom_call_target="tpu_custom_call" | custom-call | bytes 1048576 | tf_op jit(solution)/shard_map/add_kept/pallas_call | solution.py:549
  13.4 0.3 %collective-permute-done.3.packed = f32[120,128]{1,0:T(8,128)S(1)} collective-permute-done((f32[120,128]{1,0:T(8,128)S(1)}, f32[120,128]{1,0:T(8,128)S(1)}, u32[]{:S(2)}, u32[]{:S(2)}) %collective-permute-start.3) | collective-permute-done | bytes 61472 | tf_op jit(solution)/shard_map/ppermute | solution.py:626
  13.6 0.9 %add_swapped.1 = f32[32,32,128]{2,1,0:T(8,128)} custom-call(f32[32,32,128]{2,1,0:T(8,128)S(1)} %add_kept.1.own, f32[120,128]{1,0:T(8,128)S(1)} %collective-permute-done.3.packed), custom_call_target="tpu_custom_call" | custom-call | bytes 1048576 | tf_op jit(solution)/shard_map/add_swapped/pallas_call | solution.py:549
  (1 shorter events, 0.0 us)
Async XLA Ops:
  0.0 1.7 %copy-start = (f32[32,32,128]{2,1,0:T(8,128)S(1)}, f32[32,32,128]{2,1,0:T(8,128)}, u32[]{:S(2)}) copy-start(f32[32,32,128]{2,1,0:T(8,128)} %velocity.1) | copy-start | bytes 1572868
  0.0 2.2 %collective-permute-start = (f32[32,32,128]{2,1,0:T(8,128)}, f32[32,32,128]{2,1,0:T(8,128)S(1)}, u32[]{:S(2)}, u32[]{:S(2)}) collective-permute-start(f32[32,32,128]{2,1,0:T(8,128)} %velocity.1), channel_id=1, source_target_pairs={{0,1},{1,0},{2,3},{3,2},{4,5},{5,4},{6,7},{7,6},{8,9},{9,8},{10,11... | collective-permute-start | bytes 1572872 | tf_op jit(solution)/shard_map/ppermute | solution.py:570
  3.4 8.8 %collective-permute-start.1 = (f32[224,128]{1,0:T(8,128)S(1)}, f32[224,128]{1,0:T(8,128)S(1)}, u32[]{:S(2)}, u32[]{:S(2)}) collective-permute-start(f32[224,128]{1,0:T(8,128)S(1)} %get-tuple-element.19), channel_id=1, source_target_pairs={{0,2},{1,31},{2,4},{3,0},{4,6},{5,3},{6,8},{7,5},{8,10},{9,7},{10,... | collective-permute-start | bytes 344072 | tf_op jit(solution)/shard_map/ppermute | solution.py:621
  6.3 5.9 %collective-permute-start.2 = (f32[16,128]{1,0:T(8,128)S(1)}, f32[16,128]{1,0:T(8,128)S(1)}, u32[]{:S(2)}, u32[]{:S(2)}) collective-permute-start(f32[16,128]{1,0:T(8,128)S(1)} %get-tuple-element.20), channel_id=1, source_target_pairs={{1,4},{0,29},{2,6},{3,31},{4,8},{5,1},{6,10},{7,3},{8,12},{9,5},{1... | collective-permute-start | bytes 24584 | tf_op jit(solution)/shard_map/ppermute | solution.py:621
  12.2 1.5 %collective-permute-start.3 = (f32[120,128]{1,0:T(8,128)S(1)}, f32[120,128]{1,0:T(8,128)S(1)}, u32[]{:S(2)}, u32[]{:S(2)}) collective-permute-start(f32[120,128]{1,0:T(8,128)S(1)} %pack_other.1), channel_id=1, source_target_pairs={{0,1},{1,0},{2,3},{3,2},{4,5},{5,4},{6,7},{7,6},{8,9},{9,8},{10,11... | collective-permute-start | bytes 184328 | tf_op jit(solution)/shard_map/ppermute | solution.py:626
